TPU v7x, 128 devices: a whole 4x4x4 slice. The times are simulated.
128 devices in a mesh: ty: 4 (over z), tx: 8 (over y_lo, x), mode: 4 (over y_hi, core).
Axes of the slice: x: 4, y: 4 (y_hi: 2, y_lo: 2; y = y_hi * 2 + y_lo), z: 4, core: 2. Of those that a mesh axis runs over, the one named last changes fastest.
Arguments:
- object_field: float32 [2, 2048, 2048], P(None, 'ty', 'tx')
- probe: float32 [2, 4, 512, 512], P(None, 'mode')
- amplitudes: float32 [32, 512, 512], P(('ty', 'tx')), may hold values from 0.2 to 1.5
- positions: int32 [32, 2], replicated, may hold values from 0 to 1920, as said below
- owned: int32 [32, 1], P(('ty', 'tx')), may hold values from 0 to 31, as said below
Outputs:
- object_new: float32 [2, 2048, 2048], P(None, 'ty', 'tx')
- probe_new: float32 [2, 4, 512, 512], P(None, 'mode')
Inputs may be any that keep to these rules, and one draw needn't show every extreme that they name: Every position id appears exactly once in owned. Each centre has both coordinates a multiple of 128 and lies inside the tile that owns it; the positions of one tile differ.
All inputs are finite; a program needn't handle non-finite values.
Results may differ from a plain program's by a relative error of at most 0.0003.
Values sent between devices are 32-bit elements; how exact they have to be, the bound alone decides.
No kernel may reach another device: no remote copies, remote signals or barrier semaphores. Data moves between devices by JAX's collectives and lax.ppermute only.
A program may use at most 128 MiB of HBM per device.

v0:
```python
import functools

import jax
import jax.numpy as jnp
import numpy as np
from jax import lax
from jax.experimental import pallas as pl
from jax.experimental.pallas import tpu as pltpu
from jax.sharding import PartitionSpec as P

PR = 512
HALF = 256
F32 = jnp.float32
BF16 = jnp.bfloat16
MIB = 1 << 20

ROW, COL, ROW_LEFT, ROW_RIGHT, X, Z, YL, YH, CORE = range(9)


def split_np(matrix):
    high = matrix.astype(jnp.bfloat16)
    low = (matrix - high.astype(np.float64)).astype(jnp.bfloat16)
    return high, low


def tables():
    k = np.arange(HALF)[:, None]
    u = np.arange(HALF)[None, :]
    out = []
    for odd in (0, 1):
        angle = 2.0 * np.pi * (((2 * k + odd) * u) % PR) / PR
        c, s = np.cos(angle) / np.sqrt(PR), np.sin(angle) / np.sqrt(PR)
        out.append(np.block([[c, s], [-s, c]]))
    even, odd = out
    parts = []
    for m in (even, odd, even.T, odd.T):
        parts.extend(split_np(np.ascontiguousarray(m)))
    return parts


def split(x):
    high = x.astype(BF16)
    return high, (x - high.astype(F32)).astype(BF16)


def dot(a, b):
    return jnp.dot(a, b, preferred_element_type=F32)


def left(mh, ml, x):
    xh, xl = split(x)
    return dot(mh[...], xh) + (dot(mh[...], xl) + dot(ml[...], xh))


def right(x, mh, ml):
    xh, xl = split(x)
    return dot(xh, mh[...]) + (dot(xl, mh[...]) + dot(xh, ml[...]))


def smem():
    return pl.BlockSpec(memory_space=pltpu.SMEM)


def vmem():
    return pl.BlockSpec(memory_space=pltpu.VMEM)


def call(kernel, sc, ins, outs, scratch=(), limit=6, flops=0):
    return pl.pallas_call(
        kernel,
        out_shape=[jax.ShapeDtypeStruct(s, F32) for s in outs],
        in_specs=[smem()] + [vmem()] * len(ins),
        out_specs=[vmem()] * len(outs),
        scratch_shapes=[pltpu.VMEM(s, F32) for s in scratch],
        compiler_params=pltpu.CompilerParams(vmem_limit_bytes=limit * MIB),
        cost_estimate=pl.CostEstimate(
            flops=flops,
            bytes_accessed=4 * sum(int(np.prod(s)) for s in outs) + sum(a.nbytes for a in ins),
            transcendentals=0,
        ),
    )(sc, *ins)


def at(start, size, unit):
    return pl.ds(pl.multiple_of(start * unit, unit), size)


def exact_parts(x):
    a = x.astype(BF16)
    rest = x - a.astype(F32)
    b = rest.astype(BF16)
    return a, b, (rest - b.astype(F32)).astype(BF16)


def order_kernel(sc, amp, out):
    core = sc[CORE]
    row = lax.broadcasted_iota(jnp.int32, (HALF, PR), 0)
    col = lax.broadcasted_iota(jnp.int32, (HALF, PR), 1)
    pick = jnp.where(col == 2 * row + core, 1.0, 0.0).astype(BF16)
    a, b, c = exact_parts(amp[...])
    rows = (dot(pick, a) + dot(pick, b)) + dot(pick, c)
    src = lax.broadcasted_iota(jnp.int32, (PR, PR), 0)
    dst = lax.broadcasted_iota(jnp.int32, (PR, PR), 1)
    want = jnp.where(dst < HALF, 2 * dst, 2 * (dst - HALF) + 1)
    move = jnp.where(src == want, 1.0, 0.0).astype(BF16)
    a, b, c = exact_parts(rows)
    out[...] = (dot(a, move) + dot(b, move)) + dot(c, move)


def first_strips_kernel(sc, up, own, down, mid, to_right, to_left, kept, strip):
    strip[0:256] = up[...]
    strip[256:768] = own[...]
    strip[768:896] = down[...]
    mid[...] = strip[at(sc[ROW], 512, 128)]
    to_right[...] = strip[at(sc[ROW_RIGHT], 512, 128)]
    to_left[...] = strip[at(sc[ROW_LEFT], 512, 128), 0:128]
    for block in range(7):
        kept[block * 64 : block * 64 + 64] = strip[at(2 * block + sc[YH], 64, 64)]


def widen_into(sc, lft, mid, rgt, out):
    @pl.when(sc[COL] == 0)
    def _():
        out[:, 0:256] = lft[...]
        out[:, 256:512] = mid[...]

    @pl.when(sc[COL] != 0)
    def _():
        out[:, 0:128] = lft[:, 128:256]
        out[:, 128:384] = mid[...]
        out[:, 384:512] = rgt[...]


def first_widen_kernel(sc, lft, mid, rgt, out):
    widen_into(sc, lft, mid, rgt, out)


def forward_tail(sc, w, p, tabs, far, keep, send, mid):
    meh, mel, moh, mol, teh, tel, toh, tol = tabs
    wr, wi = w[0], w[1]
    pr, pi = p[0], p[1]
    er = pr * wr - pi * wi
    ei = pr * wi + pi * wr
    total = jnp.concatenate([er[:HALF] + er[HALF:], ei[:HALF] + ei[HALF:]], axis=0)
    mid[0] = left(meh, mel, total)
    total = jnp.concatenate([er[:HALF] - er[HALF:], ei[:HALF] - ei[HALF:]], axis=0)
    mid[1] = left(moh, mol, total)
    core = sc[CORE]
    power = (jnp.sum(pr * pr) + jnp.sum(pi * pi)) * (1.0 / (PR * PR))
    for parity in (0, 1):
        rows = slice(parity * HALF, parity * HALF + HALF)
        yr, yi = mid[parity, 0:HALF], mid[parity, HALF:PR]
        total = jnp.concatenate([yr[:, :HALF] + yr[:, HALF:], yi[:, :HALF] + yi[:, HALF:]], axis=1)
        even = right(total, teh, tel)
        total = jnp.concatenate([yr[:, :HALF] - yr[:, HALF:], yi[:, :HALF] - yi[:, HALF:]], axis=1)
        odd = right(total, toh, tol)
        fr = jnp.concatenate([even[:, :HALF], odd[:, :HALF]], axis=1)
        fi = jnp.concatenate([even[:, HALF:], odd[:, HALF:]], axis=1)
        far[0, rows] = fr
        far[1, rows] = fi
        own = fr * fr + fi * fi

        @pl.when(core == parity)
        def _():
            keep[0:HALF] = own

        @pl.when(core != parity)
        def _():
            send[0:HALF] = own

    keep[HALF : HALF + 8] = jnp.full((8, PR), power, F32)
    send[HALF : HALF + 8] = jnp.full((8, PR), power, F32)


def forward_first_kernel(sc, mine, other, p, *rest):
    tabs, (w, far, keep, send, mid) = rest[:8], rest[8:]
    core = sc[CORE]
    w[core] = mine[...]
    w[1 - core] = other[...]
    forward_tail(sc, w, p, tabs, far, keep, send, mid)


def forward_second_kernel(sc, aa, ab, ba, bb, old, mine, got, *rest):
    tabs, (w, p, far, keep, send, mid) = rest[:8], rest[8:]
    core, yh = sc[CORE], sc[YH]
    for plane, parity, piece in (
        (core, yh, aa),
        (core, 1 - yh, ab),
        (1 - core, yh, ba),
        (1 - core, 1 - yh, bb),
    ):
        for block in range(4):
            w[plane, at(2 * block + parity, 64, 64)] = piece[block * 64 : block * 64 + 64]
    p[core] = old[core] - mine[...]
    p[1 - core] = old[1 - core] - got[...]
    forward_tail(sc, w, p, tabs, far, keep, send, mid)


FLOPS = 3 * 8 * PR**3
FIELD = (2, PR, PR)
EXT = (HALF + 8, PR)


def forward_first(sc, mine, other, p, tabs):
    return call(
        forward_first_kernel,
        sc,
        (mine, other, p, *tabs),
        (FIELD, FIELD, EXT, EXT),
        scratch=(FIELD,),
        limit=24,
        flops=FLOPS,
    )


def forward_second(sc, pieces, p, parts, tabs):
    return call(
        forward_second_kernel,
        sc,
        (*pieces, p, *parts, *tabs),
        (FIELD, FIELD, FIELD, EXT, EXT),
        scratch=(FIELD,),
        limit=24,
        flops=FLOPS,
    )


def inverse_kernel(sc, p, far, mine, other, *rest):
    tabs, (keep, send, chi, mid, weight) = rest[:8], rest[8:]
    meh, mel, moh, mol, teh, tel, toh, tol = tabs
    core = sc[CORE]
    weight[core] = mine[...]
    weight[1 - core] = other[...]
    for parity in (0, 1):
        rows = slice(parity * HALF, parity * HALF + HALF)
        yr = far[0, rows] * weight[parity]
        yi = far[1, rows] * weight[parity]
        even = right(jnp.concatenate([yr[:, :HALF], yi[:, :HALF]], axis=1), meh, mel)
        odd = right(jnp.concatenate([yr[:, HALF:], yi[:, HALF:]], axis=1), moh, mol)
        total = even + odd
        diff = even - odd
        mid[parity, 0:HALF] = jnp.concatenate([total[:, :HALF], diff[:, :HALF]], axis=1)
        mid[parity, HALF:PR] = jnp.concatenate([total[:, HALF:], diff[:, HALF:]], axis=1)
    even = left(teh, tel, mid[0])
    odd = left(toh, tol, mid[1])
    for top in (0, 1):
        rows = slice(top * HALF, top * HALF + HALF)
        both = even - odd if top else even + odd
        cr, ci = both[:HALF], both[HALF:]
        chi[0, rows] = cr
        chi[1, rows] = ci
        pr, pi = p[0, rows], p[1, rows]
        gr = pr * cr + pi * ci
        gi = pr * ci - pi * cr

        @pl.when(core == 0)
        def _():
            keep[rows] = gr
            send[rows] = gi

        @pl.when(core != 0)
        def _():
            keep[rows] = gi
            send[rows] = gr


def inverse(sc, p, far, mine, other, tabs):
    return call(
        inverse_kernel,
        sc,
        (p, far, mine, other, *tabs),
        ((PR, PR), (PR, PR), FIELD),
        scratch=(FIELD, (2, HALF, PR)),
        limit=24,
        flops=FLOPS,
    )


def probe_gradient_kernel(sc, w, chi, mine, theirs, power):
    wr, wi = w[0], w[1]
    cr, ci = chi[0], chi[1]
    gr = wr * cr + wi * ci
    gi = wr * ci - wi * cr

    @pl.when(sc[CORE] == 0)
    def _():
        mine[...] = gr
        theirs[...] = gi

    @pl.when(sc[CORE] != 0)
    def _():
        mine[...] = gi
        theirs[...] = gr

    total = (jnp.sum(wr * wr) + jnp.sum(wi * wi)) * (1.0 / (PR * PR))
    power[...] = jnp.full((8, PR), total, F32)


def halve_kernel(sc, keep, got, stay, go):
    yh = sc[YH]
    for block in range(4):
        rows = slice(block * 64, block * 64 + 64)
        here = at(2 * block + yh, 64, 64)
        there = at(2 * block + 1 - yh, 64, 64)
        stay[rows] = keep[here] + got[here]
        go[rows] = keep[there] + got[there]


def ring_place(sc):
    return jnp.where(sc[CORE] == 0, sc[X], sc[Z])


def chunk_kernel(sc, mine, got, power, *outs):
    place, core = ring_place(sc), sc[CORE]
    for d, out in enumerate(outs):
        rows = at(lax.rem(place + d, 4), 128, 128)
        out[at(core, 128, 128)] = mine[rows]
        out[at(1 - core, 128, 128)] = got[rows]
        out[256:264] = power[...]


def stage_two_kernel(sc, stay, got, c0, c1, c2, c3, lft, mid, rgt, total):
    g = stay[...] + got[...]

    @pl.when(sc[COL] == 0)
    def _():
        lft[...] = g[:, 0:256]
        mid[...] = g[:, 256:512]
        rgt[...] = jnp.zeros(rgt.shape, F32)

    @pl.when(sc[COL] != 0)
    def _():
        lft[:, 0:128] = jnp.zeros((g.shape[0], 128), F32)
        lft[:, 128:256] = g[:, 0:128]
        mid[...] = g[:, 128:384]
        rgt[...] = g[:, 384:512]

    total[...] = (c0[...] + c1[...]) + (c2[...] + c3[...])


def stage_three_kernel(sc, mid, from_right, from_left, part, got, strip, to_up, to_down, total):
    strip[...] = jnp.zeros(strip.shape, F32)
    strip[at(sc[ROW], 256, 64)] = mid[...]
    rows = at(sc[ROW_RIGHT], 256, 64)
    strip[rows] = strip[rows] + from_right[...]
    rows = at(sc[ROW_LEFT], 256, 64)
    strip[rows, 0:128] = strip[rows, 0:128] + from_left[...]
    to_up[...] = strip[0:192]
    to_down[...] = strip[256:448]
    total[...] = part[...] + got[...]


def stage_four_kernel(
    sc, old, strip, from_up, from_down, power, part, got,
    mid, to_right, to_left, new, total,
):
    z = sc[Z]
    scale = 1.0 / (2.0 * power[0:1, 0:1])
    above = jnp.where(z == 0, 0.0, 1.0)
    below = jnp.where(z == 3, 0.0, 1.0)
    new[0:128] = (old[0:128] - (strip[0:128] + from_up[0:128]) * scale) * above
    new[128:192] = old[128:192] - (strip[128:192] + from_up[128:192]) * scale
    new[192:256] = old[192:256] - strip[192:256] * scale
    new[256:384] = old[256:384] - (strip[256:384] + from_down[0:128]) * scale
    new[384:448] = (old[384:448] - (strip[384:448] + from_down[128:192]) * scale) * below
    mid[...] = new[at(sc[ROW], 256, 64)]
    to_right[...] = new[at(sc[ROW_RIGHT], 256, 64)]
    to_left[...] = new[at(sc[ROW_LEFT], 256, 64), 0:128]
    total[...] = part[...] + got[...]


def last_four_kernel(sc, old, strip, from_up, from_down, power, part, got, new, total):
    scale = 1.0 / (2.0 * power[0:1, 0:1])
    new[0:64] = old[128:192] - (strip[128:192] + from_up[128:192]) * scale
    new[64:128] = old[192:256] - strip[192:256] * scale
    new[128:256] = old[256:384] - (strip[256:384] + from_down[0:128]) * scale
    total[...] = part[...] + got[...]


def finish_sum(part, got, total):
    scale = 1.0 / (part[256:257, 0:1] + got[256:257, 0:1])
    total[...] = (part[0:256] + got[0:256]) * scale


def stage_five_kernel(sc, lft, mid, rgt, part, got, out, total):
    widen_into(sc, lft, mid, rgt, out)
    finish_sum(part, got, total)


def last_five_kernel(sc, part, got, total):
    finish_sum(part, got, total)


def collect_kernel(sc, c0, c1, c2, c3, mine, theirs):
    place, core = ring_place(sc), sc[CORE]
    for d, part in enumerate((c0, c1, c2, c3)):
        rows = at(lax.rem(place + 4 - d, 4), 128, 128)
        mine[rows] = part[at(core, 128, 128)]
        theirs[rows] = part[at(1 - core, 128, 128)]


def join_probe_kernel(sc, old, mine, got, out):
    core = sc[CORE]
    out[core] = old[core] - mine[...]
    out[1 - core] = old[1 - core] - got[...]


def join_field_kernel(sc, aa, ab, ba, bb, out):
    core, yh = sc[CORE], sc[YH]
    for block in range(4):
        rows = slice(block * 64, block * 64 + 64)
        out[core, at(2 * block + yh, 64, 64)] = aa[rows]
        out[core, at(2 * block + 1 - yh, 64, 64)] = ab[rows]
        out[1 - core, at(2 * block + yh, 64, 64)] = ba[rows]
        out[1 - core, at(2 * block + 1 - yh, 64, 64)] = bb[rows]


def swap_core(v):
    return lax.ppermute(v, "mode", [(0, 1), (1, 0), (2, 3), (3, 2)])


def swap_plane(v):
    return lax.ppermute(v, "mode", [(0, 2), (2, 0), (1, 3), (3, 1)])


def permute(v, move):
    pairs = []
    for z in range(4):
        for y in range(2):
            for x in range(4):
                for mode in range(4):
                    tx, ty, tz = move(mode % 2, x, y, z)
                    pairs.append((((z * 2 + y) * 4 + x) * 4 + mode, ((tz * 2 + ty) * 4 + tx) * 4 + mode))
    return lax.ppermute(v, ("ty", "tx", "mode"), pairs)


def ring(v, d):
    return permute(v, lambda core, x, y, z: (x, y, (z + d) % 4) if core else ((x + d) % 4, y, z))


def pair_one(v):
    return permute(v, lambda core, x, y, z: (x, 1 - y, z) if core else (x, y, z ^ 1))


def pair_two(v):
    return permute(v, lambda core, x, y, z: (x ^ 1, y, z) if core else (x, 1 - y, z))


def pair_three(v):
    return permute(v, lambda core, x, y, z: (3 - x, y, z) if core else (x, y, 3 - z))


def step(v, axis, d):
    count = {"ty": 4, "tx": 8}[axis]
    return lax.ppermute(v, axis, [(i, i + d) for i in range(count) if 0 <= i + d < count])


def gradients(sc, w, p, chi, keep, send, power, old, last):
    got = swap_core(send)
    mine, theirs, window_power = call(
        probe_gradient_kernel, sc, (w, chi), ((PR, PR), (PR, PR), (8, PR)), limit=16
    )
    other = swap_core(theirs)
    stay, go = call(halve_kernel, sc, (keep, got), ((HALF, PR), (HALF, PR)), limit=8)
    got = swap_plane(go)
    chunks = call(chunk_kernel, sc, (mine, other, window_power), ((264, PR),) * 4, limit=8)
    chunks = [chunks[0]] + [ring(chunks[d], d) for d in (1, 2, 3)]
    lft, mid, rgt, part = call(
        stage_two_kernel,
        sc,
        (stay, got, *chunks),
        ((HALF, 256), (HALF, 256), (HALF, 128), (264, PR)),
        limit=8,
    )
    from_right, from_left, got = step(lft, "tx", -1), step(rgt, "tx", 1), pair_one(part)
    strip, to_up, to_down, part = call(
        stage_three_kernel,
        sc,
        (mid, from_right, from_left, part, got),
        ((448, 256), (192, 256), (192, 256), (264, PR)),
    )
    from_up, from_down, got = step(to_down, "ty", 1), step(to_up, "ty", -1), pair_two(part)
    ins = (old, strip, from_up, from_down, power, part, got)
    if last:
        new, part = call(last_four_kernel, sc, ins, ((256, 256), (264, PR)))
        aa = new
        total = call(last_five_kernel, sc, (part, pair_three(part)), ((256, PR),))[0]
    else:
        mid, to_right, to_left, new, part = call(
            stage_four_kernel,
            sc,
            ins,
            ((256, 256), (256, 256), (256, 128), (448, 256), (264, PR)),
        )
        lft, rgt = step(to_right, "tx", 1), step(to_left, "tx", -1)
        aa, total = call(
            stage_five_kernel,
            sc,
            (lft, mid, rgt, part, pair_three(part)),
            ((256, PR), (256, PR)),
        )
    ab = swap_plane(aa)
    pieces = (aa, ab, swap_core(aa), swap_core(ab))
    chunks = (total, ring(total, 1), ring(total, 2), ring(total, 3))
    mine, theirs = call(collect_kernel, sc, chunks, ((PR, PR), (PR, PR)), limit=8)
    return pieces, (mine, swap_core(theirs)), new


def weights(amp, keep, send):
    half = keep + swap_core(send)
    total = half + swap_plane(half)
    mine = 1.0 - amp / jnp.maximum(jnp.sqrt(total[:HALF]), 1.0)
    return mine, swap_core(mine), total[HALF:]


def body(object_field, probe, amplitudes, positions, owned):
    ty, tx, mode = lax.axis_index("ty"), lax.axis_index("tx"), lax.axis_index("mode")
    tile = ty * 8 + tx
    tiles = positions[:, 0] // 512 * 8 + positions[:, 1] // 256
    row_blocks = positions[:, 0] % 512 // 128
    col_blocks = positions[:, 1] % 256 // 128

    def pick(values, which):
        return jnp.sum(jnp.where(tiles == which, values, 0))

    core = mode % 2
    sc = jnp.stack(
        [
            pick(row_blocks, tile),
            pick(col_blocks, tile),
            pick(row_blocks, tile - 1),
            pick(row_blocks, tile + 1),
            tx % 4,
            ty,
            tx // 4,
            mode // 2,
            core,
        ]
    ).astype(jnp.int32)
    tabs = [jnp.asarray(t) for t in tables()]
    p = probe[:, 0]
    amp = call(order_kernel, sc, (amplitudes[0],), ((HALF, PR),), limit=24)[0]

    plane = lax.dynamic_index_in_dim(object_field, core, 0, keepdims=False)
    up, down = step(plane[256:512], "ty", 1), step(plane[0:128], "ty", -1)
    mid, to_right, to_left, strip = call(
        first_strips_kernel,
        sc,
        (up, plane, down),
        ((512, 256), (512, 256), (512, 128), (448, 256)),
        scratch=((896, 256),),
        limit=8,
    )
    lft, rgt = step(to_right, "tx", 1), step(to_left, "tx", -1)
    mine = call(first_widen_kernel, sc, (lft, mid, rgt), ((PR, PR),))[0]

    w, far, keep, send = forward_first(sc, mine, swap_core(mine), p, tabs)
    weight, weight_other, power = weights(amp, keep, send)
    keep, send, chi = inverse(sc, p, far, weight, weight_other, tabs)
    pieces, parts, strip = gradients(sc, w, p, chi, keep, send, power, strip, False)

    w, p, far, keep, send = forward_second(sc, pieces, p, parts, tabs)
    weight, weight_other, power = weights(amp, keep, send)
    keep, send, chi = inverse(sc, p, far, weight, weight_other, tabs)
    pieces, parts, _ = gradients(sc, w, p, chi, keep, send, power, strip, True)
    out_field = call(join_field_kernel, sc, pieces, ((2, 512, 256),))[0]
    out_probe = call(join_probe_kernel, sc, (p, *parts), (FIELD,), limit=12)[0]
    return out_field, out_probe[:, None]


def solution(mesh):
    placed = (
        P(None, "ty", "tx"),
        P(None, "mode", None, None),
        P(("ty", "tx"), None, None),
        P(),
        P(("ty", "tx"), None),
    )
    return jax.shard_map(
        body,
        mesh=mesh,
        in_specs=placed,
        out_specs=(P(None, "ty", "tx"), P(None, "mode", None, None)),
        check_vma=False,
    )
```

profile of v0, /device:TPU:1, one launch (start us, length us, event | category | flops | bytes accessed | tf_op | source)
XLA Modules:
  0.0 286.7 jit_solution(16879499660858095590)
XLA Ops:
  3.2 5.1 %collective-permute-start = (f32[256,256]{1,0:T(8,128)S(1)}, f32[256,256]{1,0:T(8,128)S(1)}, u32[]{:S(2)}, u32[]{:S(2)}) collective-permute-start(f32[256,256]{1,0:T(8,128)S(1)} %dynamic-slice_bitcast_fusion.1), channel_id=1, source_target_pairs={{0,32},{32,64},{64,96},{1,33},{33,65},{65,97},{2,34},{34,66},{66,9... | collective-permute-start | bytes 786440 | tf_op jit(solution)/shard_map/ppermute | solution.py:455
  9.2 1.4 fusion.9
  10.6 2.7 stack.39.sc
  14.1 3.3 %collective-permute-start.2 = (f32[512,256]{1,0:T(8,128)S(1)}, f32[512,256]{1,0:T(8,128)S(1)}, u32[]{:S(2)}, u32[]{:S(2)}) collective-permute-start(f32[512,256]{1,0:T(8,128)S(1)} %get-tuple-element.69), channel_id=1, source_target_pairs={{0,4},{4,8},{8,12},{12,16},{16,20},{20,24},{24,28},{1,5},{5,9},{9,... | collective-permute-start | bytes 1572872 | tf_op jit(solution)/shard_map/ppermute | solution.py:455
  18.7 6.8 %collective-permute-done.3.rgt = f32[512,128]{1,0:T(8,128)S(1)} collective-permute-done((f32[512,128]{1,0:T(8,128)S(1)}, f32[512,128]{1,0:T(8,128)S(1)}, u32[]{:S(2)}, u32[]{:S(2)}) %collective-permute-start.3) | collective-permute-done | bytes 262176 | tf_op jit(solution)/shard_map/ppermute | solution.py:455
  25.4 1.8 collective-permute-done.2.lft
  27.8 2.4 collective-permute-start.4
  30.2 2.3 collective-permute-done.4.other
  35.6 5.1 %shard_map.133 = (f32[2,512,512]{2,1,0:T(8,128)S(1)}, f32[2,512,512]{2,1,0:T(8,128)S(1)}, f32[264,512]{1,0:T(8,128)S(1)}, f32[264,512]{1,0:T(8,128)S(1)}) custom-call(s32[9]{0:T(128)S(1)} %stack.39.sc, f32[512,512]{1,0:T(8,128)S(1)} %shard_map.132.mine, f32[512,512]{1,0:T(8,128)S(1)} %collective-permute-done.4.other, f32[2,512,512]{2,1,0:T(8,128)S(1)} %bitcast.55, ...), custom_call_target="tpu_custom_call" | custom-call | flops 3221225472 | bytes 13664256 | tf_op jit(solution)/shard_map/pallas_call | solution.py:69
  41.3 1.6 collective-permute-done.5
  42.9 3.0 %collective-permute-start.6 = (f32[264,512]{1,0:T(8,128)S(1)}, f32[264,512]{1,0:T(8,128)S(1)}, u32[]{:S(2)}, u32[]{:S(2)}) collective-permute-start(f32[264,512]{1,0:T(8,128)S(1)} %add.57), channel_id=1, source_target_pairs={{0,2},{2,0},{1,3},{3,1},{4,6},{6,4},{5,7},{7,5},{8,10},{10,8},{9,1... | collective-permute-start | bytes 1622024 | tf_op jit(solution)/shard_map/ppermute | solution.py:423
  45.9 1.7 shard_map.134
  47.6 10.4 %collective-permute-done.6 = f32[264,512]{1,0:T(8,128)S(1)} collective-permute-done((f32[264,512]{1,0:T(8,128)S(1)}, f32[264,512]{1,0:T(8,128)S(1)}, u32[]{:S(2)}, u32[]{:S(2)}) %collective-permute-start.6) | collective-permute-done | bytes 540704 | tf_op jit(solution)/shard_map/ppermute | solution.py:423
  59.5 1.5 collective-permute-done.7.other
  61.1 4.9 %shard_map.135 = (f32[512,512]{1,0:T(8,128)S(1)}, f32[512,512]{1,0:T(8,128)S(1)}, f32[2,512,512]{2,1,0:T(8,128)S(1)}) custom-call(s32[9]{0:T(128)S(1)} %stack.39.sc, f32[2,512,512]{2,1,0:T(8,128)S(1)} %bitcast.56, f32[2,512,512]{2,1,0:T(8,128)S(1)} %get-tuple-element.72.far, f32[256,512]{1,0:T(8,128)S(1)} %fusion.5.mine, ...), custom_call_target="tpu_custom_call" | custom-call | flops 3221225472 | bytes 13631488 | tf_op jit(solution)/shard_map/pallas_call | solution.py:69
  66.0 1.9 shard_map.137
  68.5 2.1 collective-permute-done.10.got
  71.4 2.0 collective-permute-start.11
  73.3 3.2 %collective-permute-start.12 = (f32[264,512]{1,0:T(8,128)S(1)}, f32[264,512]{1,0:T(8,128)S(1)}, u32[]{:S(2)}, u32[]{:S(2)}) collective-permute-start(f32[264,512]{1,0:T(8,128)S(1)} %get-tuple-element.86), channel_id=1, source_target_pairs={{0,8},{1,65},{2,10},{3,67},{4,12},{5,69},{6,14},{7,71},{8,0},{9,73... | collective-permute-start | bytes 1622024 | tf_op jit(solution)/shard_map/ppermute | solution.py:434
  78.0 3.0 %collective-permute-start.9 = (f32[256,512]{1,0:T(8,128)S(1)}, f32[256,512]{1,0:T(8,128)S(1)}, u32[]{:S(2)}, u32[]{:S(2)}) collective-permute-start(f32[256,512]{1,0:T(8,128)S(1)} %get-tuple-element.78), channel_id=1, source_target_pairs={{0,2},{2,0},{1,3},{3,1},{4,6},{6,4},{5,7},{7,5},{8,10},{10,8},{9,1... | collective-permute-start | bytes 1572872 | tf_op jit(solution)/shard_map/ppermute | solution.py:423
  81.0 10.9 %collective-permute-done.9.got = f32[256,512]{1,0:T(8,128)S(1)} collective-permute-done((f32[256,512]{1,0:T(8,128)S(1)}, f32[256,512]{1,0:T(8,128)S(1)}, u32[]{:S(2)}, u32[]{:S(2)}) %collective-permute-start.9) | collective-permute-done | bytes 524320 | tf_op jit(solution)/shard_map/ppermute | solution.py:423
  92.7 4.2 %collective-permute-start.16 = (f32[264,512]{1,0:T(8,128)S(1)}, f32[264,512]{1,0:T(8,128)S(1)}, u32[]{:S(2)}, u32[]{:S(2)}) collective-permute-start(f32[264,512]{1,0:T(8,128)S(1)} %get-tuple-element.91.part), channel_id=1, source_target_pairs={{0,32},{1,17},{2,34},{3,19},{4,36},{5,21},{6,38},{7,23},{8,40},{9,... | collective-permute-start | bytes 1622024 | tf_op jit(solution)/shard_map/ppermute | solution.py:434
  98.2 4.0 %collective-permute-start.15 = (f32[256,128]{1,0:T(8,128)S(1)}, f32[256,128]{1,0:T(8,128)S(1)}, u32[]{:S(2)}, u32[]{:S(2)}) collective-permute-start(f32[256,128]{1,0:T(8,128)S(1)} %get-tuple-element.90), channel_id=1, source_target_pairs={{0,4},{4,8},{8,12},{12,16},{16,20},{20,24},{24,28},{1,5},{5,9},{9,... | collective-permute-start | bytes 393224 | tf_op jit(solution)/shard_map/ppermute | solution.py:455
  102.2 3.3 %collective-permute-done.15.from_left = f32[256,128]{1,0:T(8,128)S(1)} collective-permute-done((f32[256,128]{1,0:T(8,128)S(1)}, f32[256,128]{1,0:T(8,128)S(1)}, u32[]{:S(2)}, u32[]{:S(2)}) %collective-permute-start.15) | collective-permute-done | bytes 131104 | tf_op jit(solution)/shard_map/ppermute | solution.py:455
  108.5 2.1 collective-permute-start.17
  113.2 4.1 %collective-permute-done.18.from_down = f32[192,256]{1,0:T(8,128)S(1)} collective-permute-done((f32[192,256]{1,0:T(8,128)S(1)}, f32[192,256]{1,0:T(8,128)S(1)}, u32[]{:S(2)}, u32[]{:S(2)}) %collective-permute-start.18) | collective-permute-done | bytes 196640 | tf_op jit(solution)/shard_map/ppermute | solution.py:455
  118.1 5.6 %collective-permute-start.22 = (f32[264,512]{1,0:T(8,128)S(1)}, f32[264,512]{1,0:T(8,128)S(1)}, u32[]{:S(2)}, u32[]{:S(2)}) collective-permute-start(f32[264,512]{1,0:T(8,128)S(1)} %get-tuple-element.100.part), channel_id=1, source_target_pairs={{0,96},{1,13},{2,98},{3,15},{4,100},{5,9},{6,102},{7,11},{8,104},{... | collective-permute-start | bytes 1622024 | tf_op jit(solution)/shard_map/ppermute | solution.py:434
  123.7 1.4 collective-permute-start.20
  126.4 5.6 %collective-permute-done.21.rgt = f32[256,128]{1,0:T(8,128)S(1)} collective-permute-done((f32[256,128]{1,0:T(8,128)S(1)}, f32[256,128]{1,0:T(8,128)S(1)}, u32[]{:S(2)}, u32[]{:S(2)}) %collective-permute-start.21) | collective-permute-done | bytes 131104 | tf_op jit(solution)/shard_map/ppermute | solution.py:455
  132.8 2.2 collective-permute-start.27
  135.0 2.3 collective-permute-start.23
  137.3 3.8 %collective-permute-done.28.c3 = f32[256,512]{1,0:T(8,128)S(1)} collective-permute-done((f32[256,512]{1,0:T(8,128)S(1)}, f32[256,512]{1,0:T(8,128)S(1)}, u32[]{:S(2)}, u32[]{:S(2)}) %collective-permute-start.28) | collective-permute-done | bytes 524320 | tf_op jit(solution)/shard_map/ppermute | solution.py:434
  141.1 1.4 collective-permute-done.27.c2
  142.5 5.8 %collective-permute-done.26.c1 = f32[256,512]{1,0:T(8,128)S(1)} collective-permute-done((f32[256,512]{1,0:T(8,128)S(1)}, f32[256,512]{1,0:T(8,128)S(1)}, u32[]{:S(2)}, u32[]{:S(2)}) %collective-permute-start.26) | collective-permute-done | bytes 524320 | tf_op jit(solution)/shard_map/ppermute | solution.py:434
  149.0 6.1 %collective-permute-start.29 = (f32[512,512]{1,0:T(8,128)S(1)}, f32[512,512]{1,0:T(8,128)S(1)}, u32[]{:S(2)}, u32[]{:S(2)}) collective-permute-start(f32[512,512]{1,0:T(8,128)S(1)} %get-tuple-element.104), channel_id=1, source_target_pairs={{0,1},{1,0},{2,3},{3,2},{4,5},{5,4},{6,7},{7,6},{8,9},{9,8},{10,11... | collective-permute-start | bytes 3145736 | tf_op jit(solution)/shard_map/ppermute | solution.py:419
  155.6 2.5 collective-permute-done.24.ba
  158.9 5.4 %shard_map.144 = (f32[2,512,512]{2,1,0:T(8,128)S(1)}, f32[2,512,512]{2,1,0:T(8,128)S(1)}, f32[2,512,512]{2,1,0:T(8,128)S(1)}, f32[264,512]{1,0:T(8,128)S(1)}, f32[264,512]{1,0:T(8,128)S(1)}) custom-call(s32[9]{0:T(128)S(1)} %stack.39.sc, f32[256,512]{1,0:T(8,128)S(1)} %get-tuple-element.101.aa, f32[256,512]{1,0:T(8,128)S(1)} %collective-permute-done.23.ab, ...), custom_call_target="tpu_custom_call" | custom-call | flops 3221225472 | bytes 17858560 | tf_op jit(solution)/shard_map/pallas_call | solution.py:69
  164.7 1.6 collective-permute-done.30
  166.4 2.7 collective-permute-start.31
  169.1 12.4 %collective-permute-done.31 = f32[264,512]{1,0:T(8,128)S(1)} collective-permute-done((f32[264,512]{1,0:T(8,128)S(1)}, f32[264,512]{1,0:T(8,128)S(1)}, u32[]{:S(2)}, u32[]{:S(2)}) %collective-permute-start.31) | collective-permute-done | bytes 540704 | tf_op jit(solution)/shard_map/ppermute | solution.py:423
  181.7 1.5 collective-permute-start.32
  183.2 1.5 collective-permute-done.32.other
  184.8 4.9 %shard_map.145 = (f32[512,512]{1,0:T(8,128)S(1)}, f32[512,512]{1,0:T(8,128)S(1)}, f32[2,512,512]{2,1,0:T(8,128)S(1)}) custom-call(s32[9]{0:T(128)S(1)} %stack.39.sc, f32[2,512,512]{2,1,0:T(8,128)S(1)} %get-tuple-element.105.p.old, f32[2,512,512]{2,1,0:T(8,128)S(1)} %get-tuple-element.106.far, f32[256,512]{1,0:T(8,128)S(1)} %fusion.2.mine, ...), custom_call_target="tpu_custom_call" | custom-call | flops 3221225472 | bytes 13631488 | tf_op jit(solution)/shard_map/pallas_call | solution.py:69
  189.6 1.8 shard_map.147
  192.0 2.1 collective-permute-done.35.got
  195.4 3.6 %collective-permute-start.37 = (f32[264,512]{1,0:T(8,128)S(1)}, f32[264,512]{1,0:T(8,128)S(1)}, u32[]{:S(2)}, u32[]{:S(2)}) collective-permute-start(f32[264,512]{1,0:T(8,128)S(1)} %get-tuple-element.120), channel_id=1, source_target_pairs={{0,8},{1,65},{2,10},{3,67},{4,12},{5,69},{6,14},{7,71},{8,0},{9,73... | collective-permute-start | bytes 1622024 | tf_op jit(solution)/shard_map/ppermute | solution.py:434
  199.7 2.7 collective-permute-start.34
  202.4 12.7 %collective-permute-done.34.got = f32[256,512]{1,0:T(8,128)S(1)} collective-permute-done((f32[256,512]{1,0:T(8,128)S(1)}, f32[256,512]{1,0:T(8,128)S(1)}, u32[]{:S(2)}, u32[]{:S(2)}) %collective-permute-start.34) | collective-permute-done | bytes 524320 | tf_op jit(solution)/shard_map/ppermute | solution.py:423
  217.3 4.0 %collective-permute-start.40 = (f32[256,128]{1,0:T(8,128)S(1)}, f32[256,128]{1,0:T(8,128)S(1)}, u32[]{:S(2)}, u32[]{:S(2)}) collective-permute-start(f32[256,128]{1,0:T(8,128)S(1)} %get-tuple-element.124), channel_id=1, source_target_pairs={{0,4},{4,8},{8,12},{12,16},{16,20},{20,24},{24,28},{1,5},{5,9},{9,... | collective-permute-start | bytes 393224 | tf_op jit(solution)/shard_map/ppermute | solution.py:455
  221.3 2.1 collective-permute-done.40.from_left
  223.4 1.9 collective-permute-done.39.from_right
  226.4 1.8 collective-permute-start.42
  230.8 4.1 %collective-permute-done.43.from_down = f32[192,256]{1,0:T(8,128)S(1)} collective-permute-done((f32[192,256]{1,0:T(8,128)S(1)}, f32[192,256]{1,0:T(8,128)S(1)}, u32[]{:S(2)}, u32[]{:S(2)}) %collective-permute-start.43) | collective-permute-done | bytes 196640 | tf_op jit(solution)/shard_map/ppermute | solution.py:455
  235.6 7.0 %collective-permute-start.48 = (f32[264,512]{1,0:T(8,128)S(1)}, f32[264,512]{1,0:T(8,128)S(1)}, u32[]{:S(2)}, u32[]{:S(2)}) collective-permute-start(f32[264,512]{1,0:T(8,128)S(1)} %get-tuple-element.131.part), channel_id=1, source_target_pairs={{0,96},{1,13},{2,98},{3,15},{4,100},{5,9},{6,102},{7,11},{8,104},{... | collective-permute-start | bytes 1622024 | tf_op jit(solution)/shard_map/ppermute | solution.py:434
  242.5 7.0 %collective-permute-done.48.got = f32[264,512]{1,0:T(8,128)S(1)} collective-permute-done((f32[264,512]{1,0:T(8,128)S(1)}, f32[264,512]{1,0:T(8,128)S(1)}, u32[]{:S(2)}, u32[]{:S(2)}) %collective-permute-start.48) | collective-permute-done | bytes 540704 | tf_op jit(solution)/shard_map/ppermute | solution.py:434
  250.3 1.9 collective-permute-start.50
  252.2 6.4 %collective-permute-done.51.c3 = f32[256,512]{1,0:T(8,128)S(1)} collective-permute-done((f32[256,512]{1,0:T(8,128)S(1)}, f32[256,512]{1,0:T(8,128)S(1)}, u32[]{:S(2)}, u32[]{:S(2)}) %collective-permute-start.51) | collective-permute-done | bytes 524320 | tf_op jit(solution)/shard_map/ppermute | solution.py:434
  258.6 1.6 collective-permute-done.50.c2
  260.3 5.6 %collective-permute-done.49.c1 = f32[256,512]{1,0:T(8,128)S(1)} collective-permute-done((f32[256,512]{1,0:T(8,128)S(1)}, f32[256,512]{1,0:T(8,128)S(1)}, u32[]{:S(2)}, u32[]{:S(2)}) %collective-permute-start.49) | collective-permute-done | bytes 524320 | tf_op jit(solution)/shard_map/ppermute | solution.py:434
  266.5 5.0 %collective-permute-start.52 = (f32[512,512]{1,0:T(8,128)S(1)}, f32[512,512]{1,0:T(8,128)S(1)}, u32[]{:S(2)}, u32[]{:S(2)}) collective-permute-start(f32[512,512]{1,0:T(8,128)S(1)} %get-tuple-element.133), channel_id=1, source_target_pairs={{0,1},{1,0},{2,3},{3,2},{4,5},{5,4},{6,7},{7,6},{8,9},{9,8},{10,11... | collective-permute-start | bytes 3145736 | tf_op jit(solution)/shard_map/ppermute | solution.py:419
  271.6 2.9 %collective-permute-start.45 = (f32[256,256]{1,0:T(8,128)S(1)}, f32[256,256]{1,0:T(8,128)S(1)}, u32[]{:S(2)}, u32[]{:S(2)}) collective-permute-start(f32[256,256]{1,0:T(8,128)S(1)} %get-tuple-element.130.aa), channel_id=1, source_target_pairs={{0,2},{2,0},{1,3},{3,1},{4,6},{6,4},{5,7},{7,5},{8,10},{10,8},{9,1... | collective-permute-start | bytes 786440 | tf_op jit(solution)/shard_map/ppermute | solution.py:423
  274.9 6.1 %collective-permute-done.45.ab = f32[256,256]{1,0:T(8,128)S(1)} collective-permute-done((f32[256,256]{1,0:T(8,128)S(1)}, f32[256,256]{1,0:T(8,128)S(1)}, u32[]{:S(2)}, u32[]{:S(2)}) %collective-permute-start.45) | collective-permute-done | bytes 262176 | tf_op jit(solution)/shard_map/ppermute | solution.py:423
  283.0 1.6 shard_map.152
  284.6 2.1 shard_map.155
  (111 shorter events, 39.9 us)
Async XLA Ops:
  1.9 11.5 %collective-permute-start.1 = (f32[128,256]{1,0:T(8,128)S(1)}, f32[128,256]{1,0:T(8,128)S(1)}, u32[]{:S(2)}, u32[]{:S(2)}) collective-permute-start(f32[128,256]{1,0:T(8,128)S(1)} %dynamic-slice_bitcast_fusion.2), channel_id=1, source_target_pairs={{32,0},{64,32},{96,64},{33,1},{65,33},{97,65},{34,2},{66,34},{98,6... | collective-permute-start | bytes 393224 | tf_op jit(solution)/shard_map/ppermute | solution.py:455
  3.2 29.3 %copy-start.8 = (bf16[512,512]{1,0:T(8,128)(2,1)S(1)}, bf16[512,512]{1,0:T(8,128)(2,1)}, u32[]{:S(2)}) copy-start(bf16[512,512]{1,0:T(8,128)(2,1)} %constant.148.clone.rest_3_) | copy-start | bytes 1572868
  3.2 10.1 %collective-permute-start = (f32[256,256]{1,0:T(8,128)S(1)}, f32[256,256]{1,0:T(8,128)S(1)}, u32[]{:S(2)}, u32[]{:S(2)}) collective-permute-start(f32[256,256]{1,0:T(8,128)S(1)} %dynamic-slice_bitcast_fusion.1), channel_id=1, source_target_pairs={{0,32},{32,64},{64,96},{1,33},{33,65},{65,97},{2,34},{34,66},{66,9... | collective-permute-start | bytes 786440 | tf_op jit(solution)/shard_map/ppermute | solution.py:455
  13.3 19.2 %copy-start.3 = (f32[2,1,512,512]{3,2,1,0:T(8,128)S(1)}, f32[2,1,512,512]{3,2,1,0:T(8,128)}, u32[]{:S(2)}) copy-start(f32[2,1,512,512]{3,2,1,0:T(8,128)} %param.14) | copy-start | bytes 6291460
  13.3 19.2 %copy-start.4 = (bf16[512,512]{1,0:T(8,128)(2,1)S(1)}, bf16[512,512]{1,0:T(8,128)(2,1)}, u32[]{:S(2)}) copy-start(bf16[512,512]{1,0:T(8,128)(2,1)} %constant.152.clone.rest_7_) | copy-start | bytes 1572868
  13.3 19.2 %copy-start.5 = (bf16[512,512]{1,0:T(8,128)(2,1)S(1)}, bf16[512,512]{1,0:T(8,128)(2,1)}, u32[]{:S(2)}) copy-start(bf16[512,512]{1,0:T(8,128)(2,1)} %constant.151.clone.rest_6_) | copy-start | bytes 1572868
  13.3 19.2 %copy-start.6 = (bf16[512,512]{1,0:T(8,128)(2,1)S(1)}, bf16[512,512]{1,0:T(8,128)(2,1)}, u32[]{:S(2)}) copy-start(bf16[512,512]{1,0:T(8,128)(2,1)} %constant.150.clone.rest_5_) | copy-start | bytes 1572868
  13.3 19.2 %copy-start.7 = (bf16[512,512]{1,0:T(8,128)(2,1)S(1)}, bf16[512,512]{1,0:T(8,128)(2,1)}, u32[]{:S(2)}) copy-start(bf16[512,512]{1,0:T(8,128)(2,1)} %constant.149.clone.rest_4_) | copy-start | bytes 1572868
  14.1 13.1 %collective-permute-start.2 = (f32[512,256]{1,0:T(8,128)S(1)}, f32[512,256]{1,0:T(8,128)S(1)}, u32[]{:S(2)}, u32[]{:S(2)}) collective-permute-start(f32[512,256]{1,0:T(8,128)S(1)} %get-tuple-element.69), channel_id=1, source_target_pairs={{0,4},{4,8},{8,12},{12,16},{16,20},{20,24},{24,28},{1,5},{5,9},{9,... | collective-permute-start | bytes 1572872 | tf_op jit(solution)/shard_map/ppermute | solution.py:455
  17.4 8.1 %collective-permute-start.3 = (f32[512,128]{1,0:T(8,128)S(1)}, f32[512,128]{1,0:T(8,128)S(1)}, u32[]{:S(2)}, u32[]{:S(2)}) collective-permute-start(f32[512,128]{1,0:T(8,128)S(1)} %get-tuple-element.71), channel_id=1, source_target_pairs={{4,0},{8,4},{12,8},{16,12},{20,16},{24,20},{28,24},{5,1},{9,5},{13... | collective-permute-start | bytes 786440 | tf_op jit(solution)/shard_map/ppermute | solution.py:455
  27.8 4.6 %collective-permute-start.4 = (f32[512,512]{1,0:T(8,128)S(1)}, f32[512,512]{1,0:T(8,128)S(1)}, u32[]{:S(2)}, u32[]{:S(2)}) collective-permute-start(f32[512,512]{1,0:T(8,128)S(1)} %shard_map.132.mine), channel_id=1, source_target_pairs={{0,1},{1,0},{2,3},{3,2},{4,5},{5,4},{6,7},{7,6},{8,9},{9,8},{10,11... | collective-permute-start | bytes 3145736 | tf_op jit(solution)/shard_map/ppermute | solution.py:419
  40.8 5.1 %copy-start.2 = (f32[1,512,512]{2,1,0:T(8,128)S(1)}, f32[1,512,512]{2,1,0:T(8,128)}, u32[]{:S(2)}) copy-start(f32[1,512,512]{2,1,0:T(8,128)} %param.15) | copy-start | bytes 3145732
  40.8 2.0 collective-permute-start.5
  42.9 15.1 %collective-permute-start.6 = (f32[264,512]{1,0:T(8,128)S(1)}, f32[264,512]{1,0:T(8,128)S(1)}, u32[]{:S(2)}, u32[]{:S(2)}) collective-permute-start(f32[264,512]{1,0:T(8,128)S(1)} %add.57), channel_id=1, source_target_pairs={{0,2},{2,0},{1,3},{3,1},{4,6},{6,4},{5,7},{7,5},{8,10},{10,8},{9,1... | collective-permute-start | bytes 1622024 | tf_op jit(solution)/shard_map/ppermute | solution.py:423
  45.9 15.2 %copy-start.10 = (bf16[512,512]{1,0:T(8,128)(2,1)S(1)}, bf16[512,512]{1,0:T(8,128)(2,1)}, u32[]{:S(2)}) copy-start(bf16[512,512]{1,0:T(8,128)(2,1)} %constant.147.clone.rest_2_) | copy-start | bytes 1572868
  45.9 15.2 %copy-start.12 = (bf16[512,512]{1,0:T(8,128)(2,1)S(1)}, bf16[512,512]{1,0:T(8,128)(2,1)}, u32[]{:S(2)}) copy-start(bf16[512,512]{1,0:T(8,128)(2,1)} %constant.146.clone.rest_1_) | copy-start | bytes 1572868
  45.9 15.2 %copy-start.14 = (bf16[512,512]{1,0:T(8,128)(2,1)S(1)}, bf16[512,512]{1,0:T(8,128)(2,1)}, u32[]{:S(2)}) copy-start(bf16[512,512]{1,0:T(8,128)(2,1)} %constant.145.clone.rest_0_) | copy-start | bytes 1572868
  58.3 2.8 collective-permute-start.7
  67.9 2.7 collective-permute-start.10
  68.4 9.0 %collective-permute-start.8 = (f32[512,512]{1,0:T(8,128)S(1)}, f32[512,512]{1,0:T(8,128)S(1)}, u32[]{:S(2)}, u32[]{:S(2)}) collective-permute-start(f32[512,512]{1,0:T(8,128)S(1)} %get-tuple-element.76), channel_id=1, source_target_pairs={{0,1},{1,0},{2,3},{3,2},{4,5},{5,4},{6,7},{7,6},{8,9},{9,8},{10,11... | collective-permute-start | bytes 3145736 | tf_op jit(solution)/shard_map/ppermute | solution.py:419
  71.4 20.6 %collective-permute-start.11 = (f32[264,512]{1,0:T(8,128)S(1)}, f32[264,512]{1,0:T(8,128)S(1)}, u32[]{:S(2)}, u32[]{:S(2)}) collective-permute-start(f32[264,512]{1,0:T(8,128)S(1)} %get-tuple-element.85), channel_id=1, source_target_pairs={{0,4},{1,33},{2,6},{3,35},{4,8},{5,37},{6,10},{7,39},{8,12},{9,41}... | collective-permute-start | bytes 1622024 | tf_op jit(solution)/shard_map/ppermute | solution.py:434
  73.3 18.6 %collective-permute-start.12 = (f32[264,512]{1,0:T(8,128)S(1)}, f32[264,512]{1,0:T(8,128)S(1)}, u32[]{:S(2)}, u32[]{:S(2)}) collective-permute-start(f32[264,512]{1,0:T(8,128)S(1)} %get-tuple-element.86), channel_id=1, source_target_pairs={{0,8},{1,65},{2,10},{3,67},{4,12},{5,69},{6,14},{7,71},{8,0},{9,73... | collective-permute-start | bytes 1622024 | tf_op jit(solution)/shard_map/ppermute | solution.py:434
  76.5 15.4 %collective-permute-start.13 = (f32[264,512]{1,0:T(8,128)S(1)}, f32[264,512]{1,0:T(8,128)S(1)}, u32[]{:S(2)}, u32[]{:S(2)}) collective-permute-start(f32[264,512]{1,0:T(8,128)S(1)} %get-tuple-element.87), channel_id=1, source_target_pairs={{0,12},{1,97},{2,14},{3,99},{4,0},{5,101},{6,2},{7,103},{8,4},{9,1... | collective-permute-start | bytes 1622024 | tf_op jit(solution)/shard_map/ppermute | solution.py:434
  78.0 13.9 %collective-permute-start.9 = (f32[256,512]{1,0:T(8,128)S(1)}, f32[256,512]{1,0:T(8,128)S(1)}, u32[]{:S(2)}, u32[]{:S(2)}) collective-permute-start(f32[256,512]{1,0:T(8,128)S(1)} %get-tuple-element.78), channel_id=1, source_target_pairs={{0,2},{2,0},{1,3},{3,1},{4,6},{6,4},{5,7},{7,5},{8,10},{10,8},{9,1... | collective-permute-start | bytes 1572872 | tf_op jit(solution)/shard_map/ppermute | solution.py:423
  92.7 13.8 %collective-permute-start.16 = (f32[264,512]{1,0:T(8,128)S(1)}, f32[264,512]{1,0:T(8,128)S(1)}, u32[]{:S(2)}, u32[]{:S(2)}) collective-permute-start(f32[264,512]{1,0:T(8,128)S(1)} %get-tuple-element.91.part), channel_id=1, source_target_pairs={{0,32},{1,17},{2,34},{3,19},{4,36},{5,21},{6,38},{7,23},{8,40},{9,... | collective-permute-start | bytes 1622024 | tf_op jit(solution)/shard_map/ppermute | solution.py:434
  97.0 9.6 %collective-permute-start.14 = (f32[256,256]{1,0:T(8,128)S(1)}, f32[256,256]{1,0:T(8,128)S(1)}, u32[]{:S(2)}, u32[]{:S(2)}) collective-permute-start(f32[256,256]{1,0:T(8,128)S(1)} %get-tuple-element.89), channel_id=1, source_target_pairs={{4,0},{8,4},{12,8},{16,12},{20,16},{24,20},{28,24},{5,1},{9,5},{13... | collective-permute-start | bytes 786440 | tf_op jit(solution)/shard_map/ppermute | solution.py:455
  98.2 7.3 %collective-permute-start.15 = (f32[256,128]{1,0:T(8,128)S(1)}, f32[256,128]{1,0:T(8,128)S(1)}, u32[]{:S(2)}, u32[]{:S(2)}) collective-permute-start(f32[256,128]{1,0:T(8,128)S(1)} %get-tuple-element.90), channel_id=1, source_target_pairs={{0,4},{4,8},{8,12},{12,16},{16,20},{20,24},{24,28},{1,5},{5,9},{9,... | collective-permute-start | bytes 393224 | tf_op jit(solution)/shard_map/ppermute | solution.py:455
  107.3 10.1 %collective-permute-start.19 = (f32[264,512]{1,0:T(8,128)S(1)}, f32[264,512]{1,0:T(8,128)S(1)}, u32[]{:S(2)}, u32[]{:S(2)}) collective-permute-start(f32[264,512]{1,0:T(8,128)S(1)} %get-tuple-element.95.part), channel_id=1, source_target_pairs={{0,16},{1,5},{2,18},{3,7},{4,20},{5,1},{6,22},{7,3},{8,24},{9,13},... | collective-permute-start | bytes 1622024 | tf_op jit(solution)/shard_map/ppermute | solution.py:434
  108.5 4.7 %collective-permute-start.17 = (f32[192,256]{1,0:T(8,128)S(1)}, f32[192,256]{1,0:T(8,128)S(1)}, u32[]{:S(2)}, u32[]{:S(2)}) collective-permute-start(f32[192,256]{1,0:T(8,128)S(1)} %get-tuple-element.93), channel_id=1, source_target_pairs={{0,32},{32,64},{64,96},{1,33},{33,65},{65,97},{2,34},{34,66},{66,9... | collective-permute-start | bytes 589832 | tf_op jit(solution)/shard_map/ppermute | solution.py:455
  110.7 6.7 %collective-permute-start.18 = (f32[192,256]{1,0:T(8,128)S(1)}, f32[192,256]{1,0:T(8,128)S(1)}, u32[]{:S(2)}, u32[]{:S(2)}) collective-permute-start(f32[192,256]{1,0:T(8,128)S(1)} %get-tuple-element.94), channel_id=1, source_target_pairs={{32,0},{64,32},{96,64},{33,1},{65,33},{97,65},{34,2},{66,34},{98,6... | collective-permute-start | bytes 589832 | tf_op jit(solution)/shard_map/ppermute | solution.py:455
  118.1 13.9 %collective-permute-start.22 = (f32[264,512]{1,0:T(8,128)S(1)}, f32[264,512]{1,0:T(8,128)S(1)}, u32[]{:S(2)}, u32[]{:S(2)}) collective-permute-start(f32[264,512]{1,0:T(8,128)S(1)} %get-tuple-element.100.part), channel_id=1, source_target_pairs={{0,96},{1,13},{2,98},{3,15},{4,100},{5,9},{6,102},{7,11},{8,104},{... | collective-permute-start | bytes 1622024 | tf_op jit(solution)/shard_map/ppermute | solution.py:434
  123.7 8.3 %collective-permute-start.20 = (f32[256,256]{1,0:T(8,128)S(1)}, f32[256,256]{1,0:T(8,128)S(1)}, u32[]{:S(2)}, u32[]{:S(2)}) collective-permute-start(f32[256,256]{1,0:T(8,128)S(1)} %get-tuple-element.97), channel_id=1, source_target_pairs={{0,4},{4,8},{8,12},{12,16},{16,20},{20,24},{24,28},{1,5},{5,9},{9,... | collective-permute-start | bytes 786440 | tf_op jit(solution)/shard_map/ppermute | solution.py:455
  125.1 6.9 %collective-permute-start.21 = (f32[256,128]{1,0:T(8,128)S(1)}, f32[256,128]{1,0:T(8,128)S(1)}, u32[]{:S(2)}, u32[]{:S(2)}) collective-permute-start(f32[256,128]{1,0:T(8,128)S(1)} %get-tuple-element.99), channel_id=1, source_target_pairs={{4,0},{8,4},{12,8},{16,12},{20,16},{24,20},{28,24},{5,1},{9,5},{13... | collective-permute-start | bytes 393224 | tf_op jit(solution)/shard_map/ppermute | solution.py:455
  132.7 8.4 %collective-permute-start.28 = (f32[256,512]{1,0:T(8,128)S(1)}, f32[256,512]{1,0:T(8,128)S(1)}, u32[]{:S(2)}, u32[]{:S(2)}) collective-permute-start(f32[256,512]{1,0:T(8,128)S(1)} %get-tuple-element.102.c0), channel_id=1, source_target_pairs={{0,12},{1,97},{2,14},{3,99},{4,0},{5,101},{6,2},{7,103},{8,4},{9,1... | collective-permute-start | bytes 1572872 | tf_op jit(solution)/shard_map/ppermute | solution.py:434
  132.8 9.7 %collective-permute-start.27 = (f32[256,512]{1,0:T(8,128)S(1)}, f32[256,512]{1,0:T(8,128)S(1)}, u32[]{:S(2)}, u32[]{:S(2)}) collective-permute-start(f32[256,512]{1,0:T(8,128)S(1)} %get-tuple-element.102.c0), channel_id=1, source_target_pairs={{0,8},{1,65},{2,10},{3,67},{4,12},{5,69},{6,14},{7,71},{8,0},{9,73... | collective-permute-start | bytes 1572872 | tf_op jit(solution)/shard_map/ppermute | solution.py:434
  135.0 13.3 %collective-permute-start.26 = (f32[256,512]{1,0:T(8,128)S(1)}, f32[256,512]{1,0:T(8,128)S(1)}, u32[]{:S(2)}, u32[]{:S(2)}) collective-permute-start(f32[256,512]{1,0:T(8,128)S(1)} %get-tuple-element.102.c0), channel_id=1, source_target_pairs={{0,4},{1,33},{2,6},{3,35},{4,8},{5,37},{6,10},{7,39},{8,12},{9,41}... | collective-permute-start | bytes 1572872 | tf_op jit(solution)/shard_map/ppermute | solution.py:434
  135.0 20.2 %collective-permute-start.23 = (f32[256,512]{1,0:T(8,128)S(1)}, f32[256,512]{1,0:T(8,128)S(1)}, u32[]{:S(2)}, u32[]{:S(2)}) collective-permute-start(f32[256,512]{1,0:T(8,128)S(1)} %get-tuple-element.101.aa), channel_id=1, source_target_pairs={{0,2},{2,0},{1,3},{3,1},{4,6},{6,4},{5,7},{7,5},{8,10},{10,8},{9,1... | collective-permute-start | bytes 1572872 | tf_op jit(solution)/shard_map/ppermute | solution.py:423
  149.0 9.9 %collective-permute-start.29 = (f32[512,512]{1,0:T(8,128)S(1)}, f32[512,512]{1,0:T(8,128)S(1)}, u32[]{:S(2)}, u32[]{:S(2)}) collective-permute-start(f32[512,512]{1,0:T(8,128)S(1)} %get-tuple-element.104), channel_id=1, source_target_pairs={{0,1},{1,0},{2,3},{3,2},{4,5},{5,4},{6,7},{7,6},{8,9},{9,8},{10,11... | collective-permute-start | bytes 3145736 | tf_op jit(solution)/shard_map/ppermute | solution.py:419
  155.1 3.0 %collective-permute-start.24 = (f32[256,512]{1,0:T(8,128)S(1)}, f32[256,512]{1,0:T(8,128)S(1)}, u32[]{:S(2)}, u32[]{:S(2)}) collective-permute-start(f32[256,512]{1,0:T(8,128)S(1)} %get-tuple-element.101.aa), channel_id=1, source_target_pairs={{0,1},{1,0},{2,3},{3,2},{4,5},{5,4},{6,7},{7,6},{8,9},{9,8},{10,11... | collective-permute-start | bytes 1572872 | tf_op jit(solution)/shard_map/ppermute | solution.py:419
  155.2 3.7 %collective-permute-start.25 = (f32[256,512]{1,0:T(8,128)S(1)}, f32[256,512]{1,0:T(8,128)S(1)}, u32[]{:S(2)}, u32[]{:S(2)}) collective-permute-start(f32[256,512]{1,0:T(8,128)S(1)} %collective-permute-done.23.ab), channel_id=1, source_target_pairs={{0,1},{1,0},{2,3},{3,2},{4,5},{5,4},{6,7},{7,6},{8,9},{9,8},{10,11... | collective-permute-start | bytes 1572872 | tf_op jit(solution)/shard_map/ppermute | solution.py:419
  164.3 2.0 collective-permute-start.30
  166.4 15.1 %collective-permute-start.31 = (f32[264,512]{1,0:T(8,128)S(1)}, f32[264,512]{1,0:T(8,128)S(1)}, u32[]{:S(2)}, u32[]{:S(2)}) collective-permute-start(f32[264,512]{1,0:T(8,128)S(1)} %add.59), channel_id=1, source_target_pairs={{0,2},{2,0},{1,3},{3,1},{4,6},{6,4},{5,7},{7,5},{8,10},{10,8},{9,1... | collective-permute-start | bytes 1622024 | tf_op jit(solution)/shard_map/ppermute | solution.py:423
  181.7 3.0 %collective-permute-start.32 = (f32[256,512]{1,0:T(8,128)S(1)}, f32[256,512]{1,0:T(8,128)S(1)}, u32[]{:S(2)}, u32[]{:S(2)}) collective-permute-start(f32[256,512]{1,0:T(8,128)S(1)} %fusion.2.mine), channel_id=1, source_target_pairs={{0,1},{1,0},{2,3},{3,2},{4,5},{5,4},{6,7},{7,6},{8,9},{9,8},{10,11... | collective-permute-start | bytes 1572872 | tf_op jit(solution)/shard_map/ppermute | solution.py:419
  191.4 2.7 collective-permute-start.35
  191.9 7.2 %collective-permute-start.33 = (f32[512,512]{1,0:T(8,128)S(1)}, f32[512,512]{1,0:T(8,128)S(1)}, u32[]{:S(2)}, u32[]{:S(2)}) collective-permute-start(f32[512,512]{1,0:T(8,128)S(1)} %get-tuple-element.110), channel_id=1, source_target_pairs={{0,1},{1,0},{2,3},{3,2},{4,5},{5,4},{6,7},{7,6},{8,9},{9,8},{10,11... | collective-permute-start | bytes 3145736 | tf_op jit(solution)/shard_map/ppermute | solution.py:419
  194.9 20.2 %collective-permute-start.36 = (f32[264,512]{1,0:T(8,128)S(1)}, f32[264,512]{1,0:T(8,128)S(1)}, u32[]{:S(2)}, u32[]{:S(2)}) collective-permute-start(f32[264,512]{1,0:T(8,128)S(1)} %get-tuple-element.119), channel_id=1, source_target_pairs={{0,4},{1,33},{2,6},{3,35},{4,8},{5,37},{6,10},{7,39},{8,12},{9,41}... | collective-permute-start | bytes 1622024 | tf_op jit(solution)/shard_map/ppermute | solution.py:434
  195.4 19.7 %collective-permute-start.37 = (f32[264,512]{1,0:T(8,128)S(1)}, f32[264,512]{1,0:T(8,128)S(1)}, u32[]{:S(2)}, u32[]{:S(2)}) collective-permute-start(f32[264,512]{1,0:T(8,128)S(1)} %get-tuple-element.120), channel_id=1, source_target_pairs={{0,8},{1,65},{2,10},{3,67},{4,12},{5,69},{6,14},{7,71},{8,0},{9,73... | collective-permute-start | bytes 1622024 | tf_op jit(solution)/shard_map/ppermute | solution.py:434
  199.1 16.1 %collective-permute-start.38 = (f32[264,512]{1,0:T(8,128)S(1)}, f32[264,512]{1,0:T(8,128)S(1)}, u32[]{:S(2)}, u32[]{:S(2)}) collective-permute-start(f32[264,512]{1,0:T(8,128)S(1)} %get-tuple-element.121), channel_id=1, source_target_pairs={{0,12},{1,97},{2,14},{3,99},{4,0},{5,101},{6,2},{7,103},{8,4},{9,1... | collective-permute-start | bytes 1622024 | tf_op jit(solution)/shard_map/ppermute | solution.py:434
  199.7 15.4 %collective-permute-start.34 = (f32[256,512]{1,0:T(8,128)S(1)}, f32[256,512]{1,0:T(8,128)S(1)}, u32[]{:S(2)}, u32[]{:S(2)}) collective-permute-start(f32[256,512]{1,0:T(8,128)S(1)} %get-tuple-element.112), channel_id=1, source_target_pairs={{0,2},{2,0},{1,3},{3,1},{4,6},{6,4},{5,7},{7,5},{8,10},{10,8},{9,1... | collective-permute-start | bytes 1572872 | tf_op jit(solution)/shard_map/ppermute | solution.py:423
  215.9 9.5 %collective-permute-start.41 = (f32[264,512]{1,0:T(8,128)S(1)}, f32[264,512]{1,0:T(8,128)S(1)}, u32[]{:S(2)}, u32[]{:S(2)}) collective-permute-start(f32[264,512]{1,0:T(8,128)S(1)} %get-tuple-element.125.part), channel_id=1, source_target_pairs={{0,32},{1,17},{2,34},{3,19},{4,36},{5,21},{6,38},{7,23},{8,40},{9,... | collective-permute-start | bytes 1622024 | tf_op jit(solution)/shard_map/ppermute | solution.py:434
  216.0 9.4 %collective-permute-start.39 = (f32[256,256]{1,0:T(8,128)S(1)}, f32[256,256]{1,0:T(8,128)S(1)}, u32[]{:S(2)}, u32[]{:S(2)}) collective-permute-start(f32[256,256]{1,0:T(8,128)S(1)} %get-tuple-element.123), channel_id=1, source_target_pairs={{4,0},{8,4},{12,8},{16,12},{20,16},{24,20},{28,24},{5,1},{9,5},{13... | collective-permute-start | bytes 786440 | tf_op jit(solution)/shard_map/ppermute | solution.py:455
  217.3 6.1 %collective-permute-start.40 = (f32[256,128]{1,0:T(8,128)S(1)}, f32[256,128]{1,0:T(8,128)S(1)}, u32[]{:S(2)}, u32[]{:S(2)}) collective-permute-start(f32[256,128]{1,0:T(8,128)S(1)} %get-tuple-element.124), channel_id=1, source_target_pairs={{0,4},{4,8},{8,12},{12,16},{16,20},{20,24},{24,28},{1,5},{5,9},{9,... | collective-permute-start | bytes 393224 | tf_op jit(solution)/shard_map/ppermute | solution.py:455
  226.1 8.8 %collective-permute-start.44 = (f32[264,512]{1,0:T(8,128)S(1)}, f32[264,512]{1,0:T(8,128)S(1)}, u32[]{:S(2)}, u32[]{:S(2)}) collective-permute-start(f32[264,512]{1,0:T(8,128)S(1)} %get-tuple-element.129.part), channel_id=1, source_target_pairs={{0,16},{1,5},{2,18},{3,7},{4,20},{5,1},{6,22},{7,3},{8,24},{9,13},... | collective-permute-start | bytes 1622024 | tf_op jit(solution)/shard_map/ppermute | solution.py:434
  226.4 4.4 %collective-permute-start.42 = (f32[192,256]{1,0:T(8,128)S(1)}, f32[192,256]{1,0:T(8,128)S(1)}, u32[]{:S(2)}, u32[]{:S(2)}) collective-permute-start(f32[192,256]{1,0:T(8,128)S(1)} %get-tuple-element.127), channel_id=1, source_target_pairs={{0,32},{32,64},{64,96},{1,33},{33,65},{65,97},{2,34},{34,66},{66,9... | collective-permute-start | bytes 589832 | tf_op jit(solution)/shard_map/ppermute | solution.py:455
  228.2 6.7 %collective-permute-start.43 = (f32[192,256]{1,0:T(8,128)S(1)}, f32[192,256]{1,0:T(8,128)S(1)}, u32[]{:S(2)}, u32[]{:S(2)}) collective-permute-start(f32[192,256]{1,0:T(8,128)S(1)} %get-tuple-element.128), channel_id=1, source_target_pairs={{32,0},{64,32},{96,64},{33,1},{65,33},{97,65},{34,2},{66,34},{98,6... | collective-permute-start | bytes 589832 | tf_op jit(solution)/shard_map/ppermute | solution.py:455
  235.6 14.0 %collective-permute-start.48 = (f32[264,512]{1,0:T(8,128)S(1)}, f32[264,512]{1,0:T(8,128)S(1)}, u32[]{:S(2)}, u32[]{:S(2)}) collective-permute-start(f32[264,512]{1,0:T(8,128)S(1)} %get-tuple-element.131.part), channel_id=1, source_target_pairs={{0,96},{1,13},{2,98},{3,15},{4,100},{5,9},{6,102},{7,11},{8,104},{... | collective-permute-start | bytes 1622024 | tf_op jit(solution)/shard_map/ppermute | solution.py:434
  250.2 8.4 %collective-permute-start.51 = (f32[256,512]{1,0:T(8,128)S(1)}, f32[256,512]{1,0:T(8,128)S(1)}, u32[]{:S(2)}, u32[]{:S(2)}) collective-permute-start(f32[256,512]{1,0:T(8,128)S(1)} %shard_map.153.c0), channel_id=1, source_target_pairs={{0,12},{1,97},{2,14},{3,99},{4,0},{5,101},{6,2},{7,103},{8,4},{9,1... | collective-permute-start | bytes 1572872 | tf_op jit(solution)/shard_map/ppermute | solution.py:434
  250.3 10.0 %collective-permute-start.50 = (f32[256,512]{1,0:T(8,128)S(1)}, f32[256,512]{1,0:T(8,128)S(1)}, u32[]{:S(2)}, u32[]{:S(2)}) collective-permute-start(f32[256,512]{1,0:T(8,128)S(1)} %shard_map.153.c0), channel_id=1, source_target_pairs={{0,8},{1,65},{2,10},{3,67},{4,12},{5,69},{6,14},{7,71},{8,0},{9,73... | collective-permute-start | bytes 1572872 | tf_op jit(solution)/shard_map/ppermute | solution.py:434
  252.2 13.6 %collective-permute-start.49 = (f32[256,512]{1,0:T(8,128)S(1)}, f32[256,512]{1,0:T(8,128)S(1)}, u32[]{:S(2)}, u32[]{:S(2)}) collective-permute-start(f32[256,512]{1,0:T(8,128)S(1)} %shard_map.153.c0), channel_id=1, source_target_pairs={{0,4},{1,33},{2,6},{3,35},{4,8},{5,37},{6,10},{7,39},{8,12},{9,41}... | collective-permute-start | bytes 1572872 | tf_op jit(solution)/shard_map/ppermute | solution.py:434
  266.5 18.0 %collective-permute-start.52 = (f32[512,512]{1,0:T(8,128)S(1)}, f32[512,512]{1,0:T(8,128)S(1)}, u32[]{:S(2)}, u32[]{:S(2)}) collective-permute-start(f32[512,512]{1,0:T(8,128)S(1)} %get-tuple-element.133), channel_id=1, source_target_pairs={{0,1},{1,0},{2,3},{3,2},{4,5},{5,4},{6,7},{7,6},{8,9},{9,8},{10,11... | collective-permute-start | bytes 3145736 | tf_op jit(solution)/shard_map/ppermute | solution.py:419
  271.6 9.4 %collective-permute-start.45 = (f32[256,256]{1,0:T(8,128)S(1)}, f32[256,256]{1,0:T(8,128)S(1)}, u32[]{:S(2)}, u32[]{:S(2)}) collective-permute-start(f32[256,256]{1,0:T(8,128)S(1)} %get-tuple-element.130.aa), channel_id=1, source_target_pairs={{0,2},{2,0},{1,3},{3,1},{4,6},{6,4},{5,7},{7,5},{8,10},{10,8},{9,1... | collective-permute-start | bytes 786440 | tf_op jit(solution)/shard_map/ppermute | solution.py:423
  274.5 7.3 %collective-permute-start.46 = (f32[256,256]{1,0:T(8,128)S(1)}, f32[256,256]{1,0:T(8,128)S(1)}, u32[]{:S(2)}, u32[]{:S(2)}) collective-permute-start(f32[256,256]{1,0:T(8,128)S(1)} %get-tuple-element.130.aa), channel_id=1, source_target_pairs={{0,1},{1,0},{2,3},{3,2},{4,5},{5,4},{6,7},{7,6},{8,9},{9,8},{10,11... | collective-permute-start | bytes 786440 | tf_op jit(solution)/shard_map/ppermute | solution.py:419
  281.0 2.0 collective-permute-start.47
  284.6 2.1 copy-start.1
  (4 other events, 4.4 us)
where the time goes:
time: 287 us
  waiting for transfers between devices  135 us (47%)
  starting transfers between devices  100 us (35%)
  Pallas kernels  40.4 us (14%)
  local copies, waits for them, and re-layouts  7.14 us (2%)
  other arithmetic  2.92 us (1%)
    ppermute x6, waiting for transfers between devices, swap_plane(): return lax.ppermute(v, 'mode', [(0, 2), (2, 0), (1, 3), (3, 1)])  52.5 us
    pallas_call x25, Pallas kernels, call(): pl.pallas_call(kernel, out_shape=[jax.ShapeDtypeStruct(s, F32) for s in o...  40.4 us
    ppermute x14, waiting for transfers between devices, step(): lax.ppermute(v, axis, [(i, i + d) for i in range(count) if 0 <= i + d < c...  33.4 us
    ppermute x18, starting transfers between devices, permute(): return lax.ppermute(v, ('ty', 'tx', 'mode'), pairs)  32.9 us
    ppermute x18, waiting for transfers between devices, permute(): return lax.ppermute(v, ('ty', 'tx', 'mode'), pairs)  31.7 us
    ppermute x14, starting transfers between devices, step(): lax.ppermute(v, axis, [(i, i + d) for i in range(count) if 0 <= i + d < c...  30.7 us
    ppermute x15, starting transfers between devices, swap_core(): return lax.ppermute(v, 'mode', [(0, 1), (1, 0), (2, 3), (3, 2)])  20.1 us
    ppermute x15, waiting for transfers between devices, swap_core(): return lax.ppermute(v, 'mode', [(0, 1), (1, 0), (2, 3), (3, 2)])  17.2 us
  transfers between devices with their start and end apart: 53, of which 33 were waited for; matrix products, arithmetic and copies ran while one was open for 2% of the time, Pallas kernels for 2%

commit v1 on v0

--- a/solution.py
+++ b/solution.py
@@ -57,6 +57,14 @@
     return dot(xh, mh[...]) + (dot(xl, mh[...]) + dot(xh, ml[...]))
 
 
+def right_t(x, mh, ml):
+    def dot_t(a, b):
+        return lax.dot_general(a, b, (((1,), (1,)), ((), ())), preferred_element_type=F32)
+
+    xh, xl = split(x)
+    return dot_t(xh, mh[...]) + (dot_t(xl, mh[...]) + dot_t(xh, ml[...]))
+
+
 def smem():
     return pl.BlockSpec(memory_space=pltpu.SMEM)
 
@@ -65,11 +73,37 @@
     return pl.BlockSpec(memory_space=pltpu.VMEM)
 
 
-def call(kernel, sc, ins, outs, scratch=(), limit=6, flops=0):
+def even_row(sc):
+    return lax.rem(sc[Z], 2) == 0
+
+
+def row_sides(sc, got_first, got_second):
+    even = even_row(sc)
+    return jnp.where(even, got_second, got_first), jnp.where(even, got_first, got_second)
+
+
+def row_sends(sc, to_up, to_down, first, second):
+    @pl.when(even_row(sc))
+    def _():
+        first[...] = to_down
+        second[...] = to_up
+
+    @pl.when(jnp.logical_not(even_row(sc)))
+    def _():
+        first[...] = to_up
+        second[...] = to_down
+
+
+def call(kernel, sc, ins, outs, scratch=(), limit=6, flops=0, after=()):
+    count = len(ins)
+
+    def run(sc_ref, *refs):
+        kernel(sc_ref, *refs[:count], *refs[count + len(after) :])
+
     return pl.pallas_call(
-        kernel,
+        run,
         out_shape=[jax.ShapeDtypeStruct(s, F32) for s in outs],
-        in_specs=[smem()] + [vmem()] * len(ins),
+        in_specs=[smem()] + [vmem()] * count + [pl.BlockSpec(memory_space=pl.ANY)] * len(after),
         out_specs=[vmem()] * len(outs),
         scratch_shapes=[pltpu.VMEM(s, F32) for s in scratch],
         compiler_params=pltpu.CompilerParams(vmem_limit_bytes=limit * MIB),
@@ -78,7 +112,7 @@
             bytes_accessed=4 * sum(int(np.prod(s)) for s in outs) + sum(a.nbytes for a in ins),
             transcendentals=0,
         ),
-    )(sc, *ins)
+    )(sc, *ins, *after)
 
 
 def at(start, size, unit):
@@ -118,25 +152,23 @@
         kept[block * 64 : block * 64 + 64] = strip[at(2 * block + sc[YH], 64, 64)]
 
 
-def widen_into(sc, lft, mid, rgt, out):
+def widen_kernel(sc, lft, mid, rgt, out):
+    column = 4 * sc[YL] + sc[X]
+
     @pl.when(sc[COL] == 0)
     def _():
-        out[:, 0:256] = lft[...]
+        out[:, 0:256] = jnp.where(column == 0, 0.0, lft[...])
         out[:, 256:512] = mid[...]
 
     @pl.when(sc[COL] != 0)
     def _():
-        out[:, 0:128] = lft[:, 128:256]
+        out[:, 0:128] = jnp.where(column == 0, 0.0, lft[:, 128:256])
         out[:, 128:384] = mid[...]
-        out[:, 384:512] = rgt[...]
-
-
-def first_widen_kernel(sc, lft, mid, rgt, out):
-    widen_into(sc, lft, mid, rgt, out)
+        out[:, 384:512] = jnp.where(column == 7, 0.0, rgt[...])
 
 
 def forward_tail(sc, w, p, tabs, far, keep, send, mid):
-    meh, mel, moh, mol, teh, tel, toh, tol = tabs
+    meh, mel, moh, mol = tabs
     wr, wi = w[0], w[1]
     pr, pi = p[0], p[1]
     er = pr * wr - pi * wi
@@ -151,9 +183,9 @@
         rows = slice(parity * HALF, parity * HALF + HALF)
         yr, yi = mid[parity, 0:HALF], mid[parity, HALF:PR]
         total = jnp.concatenate([yr[:, :HALF] + yr[:, HALF:], yi[:, :HALF] + yi[:, HALF:]], axis=1)
-        even = right(total, teh, tel)
+        even = right_t(total, meh, mel)
         total = jnp.concatenate([yr[:, :HALF] - yr[:, HALF:], yi[:, :HALF] - yi[:, HALF:]], axis=1)
-        odd = right(total, toh, tol)
+        odd = right_t(total, moh, mol)
         fr = jnp.concatenate([even[:, :HALF], odd[:, :HALF]], axis=1)
         fi = jnp.concatenate([even[:, HALF:], odd[:, HALF:]], axis=1)
         far[0, rows] = fr
@@ -173,7 +205,7 @@
 
 
 def forward_first_kernel(sc, mine, other, p, *rest):
-    tabs, (w, far, keep, send, mid) = rest[:8], rest[8:]
+    tabs, (w, far, keep, send, mid) = rest[:4], rest[4:]
     core = sc[CORE]
     w[core] = mine[...]
     w[1 - core] = other[...]
@@ -181,7 +213,7 @@
 
 
 def forward_second_kernel(sc, aa, ab, ba, bb, old, mine, got, *rest):
-    tabs, (w, p, far, keep, send, mid) = rest[:8], rest[8:]
+    tabs, (w, p, far, keep, send, mid) = rest[:4], rest[4:]
     core, yh = sc[CORE], sc[YH]
     for plane, parity, piece in (
         (core, yh, aa),
@@ -205,7 +237,7 @@
     return call(
         forward_first_kernel,
         sc,
-        (mine, other, p, *tabs),
+        (mine, other, p, *tabs[:4]),
         (FIELD, FIELD, EXT, EXT),
         scratch=(FIELD,),
         limit=24,
@@ -217,7 +249,7 @@
     return call(
         forward_second_kernel,
         sc,
-        (*pieces, p, *parts, *tabs),
+        (*pieces, p, *parts, *tabs[:4]),
         (FIELD, FIELD, FIELD, EXT, EXT),
         scratch=(FIELD,),
         limit=24,
@@ -225,8 +257,8 @@
     )
 
 
-def inverse_kernel(sc, p, far, mine, other, *rest):
-    tabs, (keep, send, chi, mid, weight) = rest[:8], rest[8:]
+def inverse_kernel(sc, w, p, far, mine, other, *rest):
+    tabs, (keep, send, stay, go, power, mid, weight) = rest[:8], rest[8:]
     meh, mel, moh, mol, teh, tel, toh, tol = tabs
     core = sc[CORE]
     weight[core] = mine[...]
@@ -243,57 +275,41 @@
         mid[parity, HALF:PR] = jnp.concatenate([total[:, HALF:], diff[:, HALF:]], axis=1)
     even = left(teh, tel, mid[0])
     odd = left(toh, tol, mid[1])
+    squares = jnp.zeros((), F32)
     for top in (0, 1):
         rows = slice(top * HALF, top * HALF + HALF)
         both = even - odd if top else even + odd
         cr, ci = both[:HALF], both[HALF:]
-        chi[0, rows] = cr
-        chi[1, rows] = ci
         pr, pi = p[0, rows], p[1, rows]
-        gr = pr * cr + pi * ci
-        gi = pr * ci - pi * cr
-
-        @pl.when(core == 0)
-        def _():
-            keep[rows] = gr
-            send[rows] = gi
-
-        @pl.when(core != 0)
-        def _():
-            keep[rows] = gi
-            send[rows] = gr
-
-
-def inverse(sc, p, far, mine, other, tabs):
+        wr, wi = w[0, rows], w[1, rows]
+        for vr, vi, own, swap in ((pr, pi, keep, send), (wr, wi, stay, go)):
+            gr = vr * cr + vi * ci
+            gi = vr * ci - vi * cr
+
+            @pl.when(core == 0)
+            def _():
+                own[rows] = gr
+                swap[rows] = gi
+
+            @pl.when(core != 0)
+            def _():
+                own[rows] = gi
+                swap[rows] = gr
+
+        squares = squares + (jnp.sum(wr * wr) + jnp.sum(wi * wi))
+    power[...] = jnp.full((8, PR), squares * (1.0 / (PR * PR)), F32)
+
+
+def inverse(sc, w, p, far, mine, other, tabs):
     return call(
         inverse_kernel,
         sc,
-        (p, far, mine, other, *tabs),
-        ((PR, PR), (PR, PR), FIELD),
+        (w, p, far, mine, other, *tabs),
+        ((PR, PR), (PR, PR), (PR, PR), (PR, PR), (8, PR)),
         scratch=(FIELD, (2, HALF, PR)),
         limit=24,
         flops=FLOPS,
     )
-
-
-def probe_gradient_kernel(sc, w, chi, mine, theirs, power):
-    wr, wi = w[0], w[1]
-    cr, ci = chi[0], chi[1]
-    gr = wr * cr + wi * ci
-    gi = wr * ci - wi * cr
-
-    @pl.when(sc[CORE] == 0)
-    def _():
-        mine[...] = gr
-        theirs[...] = gi
-
-    @pl.when(sc[CORE] != 0)
-    def _():
-        mine[...] = gi
-        theirs[...] = gr
-
-    total = (jnp.sum(wr * wr) + jnp.sum(wi * wi)) * (1.0 / (PR * PR))
-    power[...] = jnp.full((8, PR), total, F32)
 
 
 def halve_kernel(sc, keep, got, stay, go):
@@ -319,7 +335,7 @@
         out[256:264] = power[...]
 
 
-def stage_two_kernel(sc, stay, got, c0, c1, c2, c3, lft, mid, rgt, total):
+def fold_kernel(sc, stay, got, lft, mid, rgt):
     g = stay[...] + got[...]
 
     @pl.when(sc[COL] == 0)
@@ -335,26 +351,29 @@
         mid[...] = g[:, 128:384]
         rgt[...] = g[:, 384:512]
 
+
+def ring_sum_kernel(sc, c0, c1, c2, c3, total):
     total[...] = (c0[...] + c1[...]) + (c2[...] + c3[...])
 
 
-def stage_three_kernel(sc, mid, from_right, from_left, part, got, strip, to_up, to_down, total):
+def stage_three_kernel(sc, mid, from_right, from_left, part, got, strip, first, second, total):
+    column = 4 * sc[YL] + sc[X]
     strip[...] = jnp.zeros(strip.shape, F32)
     strip[at(sc[ROW], 256, 64)] = mid[...]
     rows = at(sc[ROW_RIGHT], 256, 64)
-    strip[rows] = strip[rows] + from_right[...]
+    strip[rows] = strip[rows] + jnp.where(column == 7, 0.0, from_right[...])
     rows = at(sc[ROW_LEFT], 256, 64)
-    strip[rows, 0:128] = strip[rows, 0:128] + from_left[...]
-    to_up[...] = strip[0:192]
-    to_down[...] = strip[256:448]
+    strip[rows, 0:128] = strip[rows, 0:128] + jnp.where(column == 0, 0.0, from_left[...])
+    row_sends(sc, strip[0:192], strip[256:448], first, second)
     total[...] = part[...] + got[...]
 
 
 def stage_four_kernel(
-    sc, old, strip, from_up, from_down, power, part, got,
+    sc, old, strip, got_first, got_second, power, part, got,
     mid, to_right, to_left, new, total,
 ):
     z = sc[Z]
+    from_up, from_down = row_sides(sc, got_first[...], got_second[...])
     scale = 1.0 / (2.0 * power[0:1, 0:1])
     above = jnp.where(z == 0, 0.0, 1.0)
     below = jnp.where(z == 3, 0.0, 1.0)
@@ -369,7 +388,8 @@
     total[...] = part[...] + got[...]
 
 
-def last_four_kernel(sc, old, strip, from_up, from_down, power, part, got, new, total):
+def last_four_kernel(sc, old, strip, got_first, got_second, power, part, got, new, total):
+    from_up, from_down = row_sides(sc, got_first[...], got_second[...])
     scale = 1.0 / (2.0 * power[0:1, 0:1])
     new[0:64] = old[128:192] - (strip[128:192] + from_up[128:192]) * scale
     new[64:128] = old[192:256] - strip[192:256] * scale
@@ -377,18 +397,9 @@
     total[...] = part[...] + got[...]
 
 
-def finish_sum(part, got, total):
+def finish_sum_kernel(sc, part, got, total):
     scale = 1.0 / (part[256:257, 0:1] + got[256:257, 0:1])
     total[...] = (part[0:256] + got[0:256]) * scale
-
-
-def stage_five_kernel(sc, lft, mid, rgt, part, got, out, total):
-    widen_into(sc, lft, mid, rgt, out)
-    finish_sum(part, got, total)
-
-
-def last_five_kernel(sc, part, got, total):
-    finish_sum(part, got, total)
 
 
 def collect_kernel(sc, c0, c1, c2, c3, mine, theirs):
@@ -455,55 +466,82 @@
     return lax.ppermute(v, axis, [(i, i + d) for i in range(count) if 0 <= i + d < count])
 
 
-def gradients(sc, w, p, chi, keep, send, power, old, last):
+def shift(v, d):
+    return lax.ppermute(v, "tx", [(i, (i + d) % 8) for i in range(8)])
+
+
+def swap_rows(first, second):
+    return (
+        lax.ppermute(first, "ty", [(0, 1), (1, 0), (2, 3), (3, 2)]),
+        lax.ppermute(second, "ty", [(1, 2), (2, 1)]),
+    )
+
+
+def fold_gradients(sc, w, p, far, weight, weight_other, tabs):
+    keep, send, mine, theirs, window_power = inverse(sc, w, p, far, weight, weight_other, tabs)
     got = swap_core(send)
-    mine, theirs, window_power = call(
-        probe_gradient_kernel, sc, (w, chi), ((PR, PR), (PR, PR), (8, PR)), limit=16
-    )
     other = swap_core(theirs)
     stay, go = call(halve_kernel, sc, (keep, got), ((HALF, PR), (HALF, PR)), limit=8)
     got = swap_plane(go)
-    chunks = call(chunk_kernel, sc, (mine, other, window_power), ((264, PR),) * 4, limit=8)
+    chunks = call(
+        chunk_kernel, sc, (mine, other, window_power), ((264, PR),) * 4, limit=8, after=(go,)
+    )
     chunks = [chunks[0]] + [ring(chunks[d], d) for d in (1, 2, 3)]
-    lft, mid, rgt, part = call(
-        stage_two_kernel,
-        sc,
-        (stay, got, *chunks),
-        ((HALF, 256), (HALF, 256), (HALF, 128), (264, PR)),
-        limit=8,
-    )
-    from_right, from_left, got = step(lft, "tx", -1), step(rgt, "tx", 1), pair_one(part)
-    strip, to_up, to_down, part = call(
+    lft, mid, rgt = call(
+        fold_kernel, sc, (stay, got), ((HALF, 256), (HALF, 256), (HALF, 128)), limit=8, flops=6 * 10**9
+    )
+    part = call(ring_sum_kernel, sc, chunks, ((264, PR),), after=(lft,))[0]
+    from_right, from_left, got = shift(lft, -1), shift(rgt, 1), pair_one(part)
+    strip, first, second, part = call(
         stage_three_kernel,
         sc,
         (mid, from_right, from_left, part, got),
         ((448, 256), (192, 256), (192, 256), (264, PR)),
     )
-    from_up, from_down, got = step(to_down, "ty", 1), step(to_up, "ty", -1), pair_two(part)
-    ins = (old, strip, from_up, from_down, power, part, got)
-    if last:
-        new, part = call(last_four_kernel, sc, ins, ((256, 256), (264, PR)))
-        aa = new
-        total = call(last_five_kernel, sc, (part, pair_three(part)), ((256, PR),))[0]
-    else:
-        mid, to_right, to_left, new, part = call(
-            stage_four_kernel,
-            sc,
-            ins,
-            ((256, 256), (256, 256), (256, 128), (448, 256), (264, PR)),
-        )
-        lft, rgt = step(to_right, "tx", 1), step(to_left, "tx", -1)
-        aa, total = call(
-            stage_five_kernel,
-            sc,
-            (lft, mid, rgt, part, pair_three(part)),
-            ((256, PR), (256, PR)),
-        )
+    first, second = swap_rows(first, second)
+    return strip, first, second, part, pair_two(part)
+
+
+def spread(total):
+    return total, ring(total, 1), ring(total, 2), ring(total, 3)
+
+
+def update(sc, old, folded, power):
+    strip, first, second, part, got = folded
+    mid, to_right, to_left, new, part = call(
+        stage_four_kernel,
+        sc,
+        (old, strip, first, second, power, part, got),
+        ((256, 256), (256, 256), (256, 128), (448, 256), (264, PR)),
+    )
+    lft, rgt, got = shift(to_right, 1), shift(to_left, -1), pair_three(part)
+    aa = call(widen_kernel, sc, (lft, mid, rgt), ((256, PR),))[0]
     ab = swap_plane(aa)
+    total = call(finish_sum_kernel, sc, (part, got), ((256, PR),), after=(aa,))[0]
     pieces = (aa, ab, swap_core(aa), swap_core(ab))
-    chunks = (total, ring(total, 1), ring(total, 2), ring(total, 3))
-    mine, theirs = call(collect_kernel, sc, chunks, ((PR, PR), (PR, PR)), limit=8)
+    mine, theirs = call(
+        collect_kernel, sc, spread(total), ((PR, PR), (PR, PR)), limit=8, after=pieces[3:]
+    )
     return pieces, (mine, swap_core(theirs)), new
+
+
+def last_update(sc, p, old, folded, power):
+    strip, first, second, part, got = folded
+    aa, part = call(
+        last_four_kernel,
+        sc,
+        (old, strip, first, second, power, part, got),
+        ((256, 256), (264, PR)),
+    )
+    got = pair_three(part)
+    ab = swap_plane(aa)
+    total = call(finish_sum_kernel, sc, (part, got), ((256, PR),), after=(ab,))[0]
+    pieces = (aa, ab, swap_core(aa), swap_core(ab))
+    field = call(join_field_kernel, sc, pieces, ((2, 512, 256),))[0]
+    mine, theirs = call(
+        collect_kernel, sc, spread(total), ((PR, PR), (PR, PR)), limit=8, after=(field,)
+    )
+    return field, call(join_probe_kernel, sc, (p, mine, swap_core(theirs)), (FIELD,), limit=12)[0]
 
 
 def weights(amp, keep, send):
@@ -552,19 +590,17 @@
         limit=8,
     )
     lft, rgt = step(to_right, "tx", 1), step(to_left, "tx", -1)
-    mine = call(first_widen_kernel, sc, (lft, mid, rgt), ((PR, PR),))[0]
+    mine = call(widen_kernel, sc, (lft, mid, rgt), ((PR, PR),))[0]
 
     w, far, keep, send = forward_first(sc, mine, swap_core(mine), p, tabs)
     weight, weight_other, power = weights(amp, keep, send)
-    keep, send, chi = inverse(sc, p, far, weight, weight_other, tabs)
-    pieces, parts, strip = gradients(sc, w, p, chi, keep, send, power, strip, False)
+    folded = fold_gradients(sc, w, p, far, weight, weight_other, tabs)
+    pieces, parts, strip = update(sc, strip, folded, power)
 
     w, p, far, keep, send = forward_second(sc, pieces, p, parts, tabs)
     weight, weight_other, power = weights(amp, keep, send)
-    keep, send, chi = inverse(sc, p, far, weight, weight_other, tabs)
-    pieces, parts, _ = gradients(sc, w, p, chi, keep, send, power, strip, True)
-    out_field = call(join_field_kernel, sc, pieces, ((2, 512, 256),))[0]
-    out_probe = call(join_probe_kernel, sc, (p, *parts), (FIELD,), limit=12)[0]
+    folded = fold_gradients(sc, w, p, far, weight, weight_other, tabs)
+    out_field, out_probe = last_update(sc, p, strip, folded, power)
     return out_field, out_probe[:, None]
 
 

time: 287 us -> 279 us (0.972); the launches traced: 287 us -> 276 us
  starting transfers between devices: 100 us -> 78.7 us
  Pallas kernels: 40.4 us -> 51.7 us
    ppermute x14 -> x4, waiting for transfers between devices: 33.4 us -> 8.45 us  [step(): lax.ppermute(v, axis, [(i, i + d) for i in range(count) if 0 <= i + d < c...]
    ppermute x14 -> x4, starting transfers between devices: 30.7 us -> 10.8 us  [step(): lax.ppermute(v, axis, [(i, i + d) for i in range(count) if 0 <= i + d < c...]
    ppermute x0 -> x10, waiting for transfers between devices: none -> 19.9 us  [the longest x6 14.9 us: shift(): return lax.ppermute(v, 'tx', [(i, (i + d) % 8) for i in range(8)])]
    ppermute x18, waiting for transfers between devices: 31.7 us -> 45.8 us  [permute(): return lax.ppermute(v, ('ty', 'tx', 'mode'), pairs)]
    ppermute x0 -> x10, starting transfers between devices: none -> 12 us  [the longest x6 7.84 us: shift(): return lax.ppermute(v, 'tx', [(i, (i + d) % 8) for i in range(8)])]
    pallas_call x25 -> x26, Pallas kernels: 40.4 us -> 51.7 us  [call(): pl.pallas_call(run, out_shape=[jax.ShapeDtypeStruct(s, F32) for s in outs...]
    ppermute x6, waiting for transfers between devices: 52.5 us -> 42.4 us  [swap_plane(): return lax.ppermute(v, 'mode', [(0, 2), (2, 0), (1, 3), (3, 1)])]
    ppermute x15, starting transfers between devices: 20.1 us -> 13 us  [swap_core(): return lax.ppermute(v, 'mode', [(0, 1), (1, 0), (2, 3), (3, 2)])]
  transfers between devices with their start and end apart: 53 -> 53, of which waited for: 33 -> 39; matrix products, arithmetic and copies ran while one was open for 2% -> 2% of each run, Pallas kernels for 2% -> 3%
where the time goes in v1:
time: 279 us; the launch traced here: 276 us
  waiting for transfers between devices  136 us (49%)
  starting transfers between devices  78.7 us (28%)
  Pallas kernels  51.7 us (19%)
  local copies, waits for them, and re-layouts  5.11 us (2%)
  other arithmetic  2.9 us (1%)
    pallas_call x26, Pallas kernels, call(): pl.pallas_call(run, out_shape=[jax.ShapeDtypeStruct(s, F32) for s in outs...  51.7 us
    ppermute x18, waiting for transfers between devices, permute(): return lax.ppermute(v, ('ty', 'tx', 'mode'), pairs)  45.8 us
    ppermute x6, waiting for transfers between devices, swap_plane(): return lax.ppermute(v, 'mode', [(0, 2), (2, 0), (1, 3), (3, 1)])  42.4 us
    ppermute x18, starting transfers between devices, permute(): return lax.ppermute(v, ('ty', 'tx', 'mode'), pairs)  30.7 us
    ppermute x15, waiting for transfers between devices, swap_core(): return lax.ppermute(v, 'mode', [(0, 1), (1, 0), (2, 3), (3, 2)])  19.4 us
    ppermute x6, waiting for transfers between devices, shift(): return lax.ppermute(v, 'tx', [(i, (i + d) % 8) for i in range(8)])  14.9 us
    ppermute x15, starting transfers between devices, swap_core(): return lax.ppermute(v, 'mode', [(0, 1), (1, 0), (2, 3), (3, 2)])  13 us
    ppermute x6, starting transfers between devices, swap_plane(): return lax.ppermute(v, 'mode', [(0, 2), (2, 0), (1, 3), (3, 1)])  12.3 us
  transfers between devices with their start and end apart: 53, of which 39 were waited for; matrix products, arithmetic and copies ran while one was open for 2% of the time, Pallas kernels for 3%

profile of v1, /device:TPU:1, one launch (start us, length us, event | category | flops | bytes accessed | tf_op | source)
XLA Modules:
  0.0 275.7 jit_solution(1792165322928813422)
XLA Ops:
  3.2 5.0 %collective-permute-start = (f32[256,256]{1,0:T(8,128)S(1)}, f32[256,256]{1,0:T(8,128)S(1)}, u32[]{:S(2)}, u32[]{:S(2)}) collective-permute-start(f32[256,256]{1,0:T(8,128)S(1)} %dynamic-slice_bitcast_fusion.1), channel_id=1, source_target_pairs={{0,32},{32,64},{64,96},{1,33},{33,65},{65,97},{2,34},{34,66},{66,9... | collective-permute-start | bytes 786440 | tf_op jit(solution)/shard_map/ppermute | solution.py:466
  9.0 1.4 fusion.9
  10.4 2.5 stack.39.sc_ref
  13.9 3.2 %collective-permute-start.2 = (f32[512,256]{1,0:T(8,128)S(1)}, f32[512,256]{1,0:T(8,128)S(1)}, u32[]{:S(2)}, u32[]{:S(2)}) collective-permute-start(f32[512,256]{1,0:T(8,128)S(1)} %get-tuple-element.63), channel_id=1, source_target_pairs={{0,4},{4,8},{8,12},{12,16},{16,20},{20,24},{24,28},{1,5},{5,9},{9,... | collective-permute-start | bytes 1572872 | tf_op jit(solution)/shard_map/ppermute | solution.py:466
  18.4 6.6 %collective-permute-done.3.refs_2_ = f32[512,128]{1,0:T(8,128)S(1)} collective-permute-done((f32[512,128]{1,0:T(8,128)S(1)}, f32[512,128]{1,0:T(8,128)S(1)}, u32[]{:S(2)}, u32[]{:S(2)}) %collective-permute-start.3) | collective-permute-done | bytes 262176 | tf_op jit(solution)/shard_map/ppermute | solution.py:466
  25.0 1.8 collective-permute-done.2.refs_0_
  27.4 2.5 collective-permute-start.4
  29.9 2.3 collective-permute-done.4.refs_1_
  32.2 5.2 %shard_map.133 = (f32[2,512,512]{2,1,0:T(8,128)S(1)}, f32[2,512,512]{2,1,0:T(8,128)S(1)}, f32[264,512]{1,0:T(8,128)S(1)}, f32[264,512]{1,0:T(8,128)S(1)}) custom-call(s32[9]{0:T(128)S(1)} %stack.39.sc_ref, f32[512,512]{1,0:T(8,128)S(1)} %shard_map.132.refs_0_, f32[512,512]{1,0:T(8,128)S(1)} %collective-permute-done.4.refs_1_, f32[2,512,512]{2,1,0:T(8,128)S(1)} %bitcast.55, ...), custom_call_target="tpu_custom_call" | custom-call | flops 3221225472 | bytes 11567104 | tf_op jit(solution)/shard_map/pallas_call | solution.py:103
  37.8 1.6 collective-permute-done.5
  39.5 3.0 %collective-permute-start.6 = (f32[264,512]{1,0:T(8,128)S(1)}, f32[264,512]{1,0:T(8,128)S(1)}, u32[]{:S(2)}, u32[]{:S(2)}) collective-permute-start(f32[264,512]{1,0:T(8,128)S(1)} %add.57), channel_id=1, source_target_pairs={{0,2},{2,0},{1,3},{3,1},{4,6},{6,4},{5,7},{7,5},{8,10},{10,8},{9,1... | collective-permute-start | bytes 1622024 | tf_op jit(solution)/shard_map/ppermute | solution.py:434
  42.5 1.7 shard_map.134
  44.2 10.4 %collective-permute-done.6 = f32[264,512]{1,0:T(8,128)S(1)} collective-permute-done((f32[264,512]{1,0:T(8,128)S(1)}, f32[264,512]{1,0:T(8,128)S(1)}, u32[]{:S(2)}, u32[]{:S(2)}) %collective-permute-start.6) | collective-permute-done | bytes 540704 | tf_op jit(solution)/shard_map/ppermute | solution.py:434
  56.1 1.5 collective-permute-done.7.refs_4_
  57.7 6.5 %shard_map.135 = (f32[512,512]{1,0:T(8,128)S(1)}, f32[512,512]{1,0:T(8,128)S(1)}, f32[512,512]{1,0:T(8,128)S(1)}, f32[512,512]{1,0:T(8,128)S(1)}, f32[8,512]{1,0:T(8,128)S(1)}) custom-call(s32[9]{0:T(128)S(1)} %stack.39.sc_ref, f32[2,512,512]{2,1,0:T(8,128)S(1)} %get-tuple-element.66.refs_0_, f32[2,512,512]{2,1,0:T(8,128)S(1)} %bitcast.56, ...), custom_call_target="tpu_custom_call" | custom-call | flops 3221225472 | bytes 15745024 | tf_op jit(solution)/shard_map/pallas_call | solution.py:103
  64.8 2.1 collective-permute-done.8.refs_1_
  67.6 3.0 %collective-permute-start.9 = (f32[256,512]{1,0:T(8,128)S(1)}, f32[256,512]{1,0:T(8,128)S(1)}, u32[]{:S(2)}, u32[]{:S(2)}) collective-permute-start(f32[256,512]{1,0:T(8,128)S(1)} %get-tuple-element.73.refs_3_), channel_id=1, source_target_pairs={{0,2},{2,0},{1,3},{3,1},{4,6},{6,4},{5,7},{7,5},{8,10},{10,8},{9,1... | collective-permute-start | bytes 1572872 | tf_op jit(solution)/shard_map/ppermute | solution.py:434
  71.3 2.1 collective-permute-start.13
  73.4 3.2 %collective-permute-start.14 = (f32[264,512]{1,0:T(8,128)S(1)}, f32[264,512]{1,0:T(8,128)S(1)}, u32[]{:S(2)}, u32[]{:S(2)}) collective-permute-start(f32[264,512]{1,0:T(8,128)S(1)} %get-tuple-element.82), channel_id=1, source_target_pairs={{0,8},{1,65},{2,10},{3,67},{4,12},{5,69},{6,14},{7,71},{8,0},{9,73... | collective-permute-start | bytes 1622024 | tf_op jit(solution)/shard_map/ppermute | solution.py:445
  77.5 4.9 %collective-permute-done.9.refs_1_ = f32[256,512]{1,0:T(8,128)S(1)} collective-permute-done((f32[256,512]{1,0:T(8,128)S(1)}, f32[256,512]{1,0:T(8,128)S(1)}, u32[]{:S(2)}, u32[]{:S(2)}) %collective-permute-start.9) | collective-permute-done | bytes 524320 | tf_op jit(solution)/shard_map/ppermute | solution.py:434
  83.0 6.5 %collective-permute-done.14.refs_2_ = f32[264,512]{1,0:T(8,128)S(1)} collective-permute-done((f32[264,512]{1,0:T(8,128)S(1)}, f32[264,512]{1,0:T(8,128)S(1)}, u32[]{:S(2)}, u32[]{:S(2)}) %collective-permute-start.14) | collective-permute-done | bytes 540704 | tf_op jit(solution)/shard_map/ppermute | solution.py:445
  90.1 3.3 %collective-permute-start.16 = (f32[264,512]{1,0:T(8,128)S(1)}, f32[264,512]{1,0:T(8,128)S(1)}, u32[]{:S(2)}, u32[]{:S(2)}) collective-permute-start(f32[264,512]{1,0:T(8,128)S(1)} %shard_map.139.refs_3_), channel_id=1, source_target_pairs={{0,32},{1,17},{2,34},{3,19},{4,36},{5,21},{6,38},{7,23},{8,40},{9,... | collective-permute-start | bytes 1622024 | tf_op jit(solution)/shard_map/ppermute | solution.py:445
  94.9 5.7 %collective-permute-done.11.refs_2_ = f32[256,128]{1,0:T(8,128)S(1)} collective-permute-done((f32[256,128]{1,0:T(8,128)S(1)}, f32[256,128]{1,0:T(8,128)S(1)}, u32[]{:S(2)}, u32[]{:S(2)}) %collective-permute-start.11) | collective-permute-done | bytes 131104 | tf_op jit(solution)/shard_map/ppermute | solution.py:470
  103.4 1.3 collective-permute-start.17
  105.4 2.6 collective-permute-done.17.refs_2_
  108.0 3.9 %collective-permute-done.19.refs_6_ = f32[264,512]{1,0:T(8,128)S(1)} collective-permute-done((f32[264,512]{1,0:T(8,128)S(1)}, f32[264,512]{1,0:T(8,128)S(1)}, u32[]{:S(2)}, u32[]{:S(2)}) %collective-permute-start.19) | collective-permute-done | bytes 540704 | tf_op jit(solution)/shard_map/ppermute | solution.py:445
  112.7 4.6 %collective-permute-start.21 = (f32[256,128]{1,0:T(8,128)S(1)}, f32[256,128]{1,0:T(8,128)S(1)}, u32[]{:S(2)}, u32[]{:S(2)}) collective-permute-start(f32[256,128]{1,0:T(8,128)S(1)} %get-tuple-element.91), channel_id=1, source_target_pairs={{0,28},{4,0},{8,4},{12,8},{16,12},{20,16},{24,20},{28,24},{1,29},{... | collective-permute-start | bytes 393224 | tf_op jit(solution)/shard_map/ppermute | solution.py:470
  119.3 1.7 collective-permute-done.20.refs_0_
  121.6 1.6 collective-permute-start.22
  123.2 6.5 %collective-permute-done.25.refs_1_ = f32[264,512]{1,0:T(8,128)S(1)} collective-permute-done((f32[264,512]{1,0:T(8,128)S(1)}, f32[264,512]{1,0:T(8,128)S(1)}, u32[]{:S(2)}, u32[]{:S(2)}) %collective-permute-start.25) | collective-permute-done | bytes 540704 | tf_op jit(solution)/shard_map/ppermute | solution.py:445
  130.4 2.2 collective-permute-start.28
  134.3 4.3 %collective-permute-start.24 = (f32[256,512]{1,0:T(8,128)S(1)}, f32[256,512]{1,0:T(8,128)S(1)}, u32[]{:S(2)}, u32[]{:S(2)}) collective-permute-start(f32[256,512]{1,0:T(8,128)S(1)} %collective-permute-done.22.refs_1_), channel_id=1, source_target_pairs={{0,1},{1,0},{2,3},{3,2},{4,5},{5,4},{6,7},{7,6},{8,9},{9,8},{10,11... | collective-permute-start | bytes 1572872 | tf_op jit(solution)/shard_map/ppermute | solution.py:430
  138.7 5.7 %collective-permute-done.28.refs_3_ = f32[256,512]{1,0:T(8,128)S(1)} collective-permute-done((f32[256,512]{1,0:T(8,128)S(1)}, f32[256,512]{1,0:T(8,128)S(1)}, u32[]{:S(2)}, u32[]{:S(2)}) %collective-permute-start.28) | collective-permute-done | bytes 524320 | tf_op jit(solution)/shard_map/ppermute | solution.py:445
  144.4 3.4 %collective-permute-done.26.refs_1_ = f32[256,512]{1,0:T(8,128)S(1)} collective-permute-done((f32[256,512]{1,0:T(8,128)S(1)}, f32[256,512]{1,0:T(8,128)S(1)}, u32[]{:S(2)}, u32[]{:S(2)}) %collective-permute-start.26) | collective-permute-done | bytes 524320 | tf_op jit(solution)/shard_map/ppermute | solution.py:445
  149.1 2.9 %collective-permute-done.23.refs_2_ = f32[256,512]{1,0:T(8,128)S(1)} collective-permute-done((f32[256,512]{1,0:T(8,128)S(1)}, f32[256,512]{1,0:T(8,128)S(1)}, u32[]{:S(2)}, u32[]{:S(2)}) %collective-permute-start.23) | collective-permute-done | bytes 524320 | tf_op jit(solution)/shard_map/ppermute | solution.py:430
  152.0 15.6 %shard_map.145 = (f32[2,512,512]{2,1,0:T(8,128)S(1)}, f32[2,512,512]{2,1,0:T(8,128)S(1)}, f32[2,512,512]{2,1,0:T(8,128)S(1)}, f32[264,512]{1,0:T(8,128)S(1)}, f32[264,512]{1,0:T(8,128)S(1)}) custom-call(s32[9]{0:T(128)S(1)} %stack.39.sc_ref, f32[256,512]{1,0:T(8,128)S(1)} %shard_map.142.refs_2_.refs_0_, f32[256,512]{1,0:T(8,128)S(1)} %collective-permute-done.22.refs_1_, ...), custom_call_target="tpu_custom_call" | custom-call | flops 3221225472 | bytes 15761408 | tf_op jit(solution)/shard_map/pallas_call | solution.py:103
  168.0 1.6 collective-permute-done.30
  169.7 1.6 collective-permute-start.31
  171.3 13.5 %collective-permute-done.31 = f32[264,512]{1,0:T(8,128)S(1)} collective-permute-done((f32[264,512]{1,0:T(8,128)S(1)}, f32[264,512]{1,0:T(8,128)S(1)}, u32[]{:S(2)}, u32[]{:S(2)}) %collective-permute-start.31) | collective-permute-done | bytes 540704 | tf_op jit(solution)/shard_map/ppermute | solution.py:434
  186.4 1.5 collective-permute-done.32.refs_4_
  187.9 6.3 %shard_map.146 = (f32[512,512]{1,0:T(8,128)S(1)}, f32[512,512]{1,0:T(8,128)S(1)}, f32[512,512]{1,0:T(8,128)S(1)}, f32[512,512]{1,0:T(8,128)S(1)}, f32[8,512]{1,0:T(8,128)S(1)}) custom-call(s32[9]{0:T(128)S(1)} %stack.39.sc_ref, f32[2,512,512]{2,1,0:T(8,128)S(1)} %get-tuple-element.95.refs_0_, f32[2,512,512]{2,1,0:T(8,128)S(1)} %get-tuple-element.96.refs_1_.refs_0_, ...), custom_call_target="tpu_custom_call" | custom-call | flops 3221225472 | bytes 15745024 | tf_op jit(solution)/shard_map/pallas_call | solution.py:103
  194.8 2.1 collective-permute-done.33.refs_1_
  197.6 1.6 collective-permute-start.34
  200.7 2.6 collective-permute-start.39
  203.4 1.4 collective-permute-start.40
  204.8 7.5 %collective-permute-done.34.refs_1_ = f32[256,512]{1,0:T(8,128)S(1)} collective-permute-done((f32[256,512]{1,0:T(8,128)S(1)}, f32[256,512]{1,0:T(8,128)S(1)}, u32[]{:S(2)}, u32[]{:S(2)}) %collective-permute-start.34) | collective-permute-done | bytes 524320 | tf_op jit(solution)/shard_map/ppermute | solution.py:434
  213.0 3.0 %collective-permute-done.39.refs_2_ = f32[264,512]{1,0:T(8,128)S(1)} collective-permute-done((f32[264,512]{1,0:T(8,128)S(1)}, f32[264,512]{1,0:T(8,128)S(1)}, u32[]{:S(2)}, u32[]{:S(2)}) %collective-permute-start.39) | collective-permute-done | bytes 540704 | tf_op jit(solution)/shard_map/ppermute | solution.py:445
  217.1 1.7 collective-permute-start.35
  218.8 6.0 %collective-permute-done.36.refs_2_ = f32[256,128]{1,0:T(8,128)S(1)} collective-permute-done((f32[256,128]{1,0:T(8,128)S(1)}, f32[256,128]{1,0:T(8,128)S(1)}, u32[]{:S(2)}, u32[]{:S(2)}) %collective-permute-start.36) | collective-permute-done | bytes 131104 | tf_op jit(solution)/shard_map/ppermute | solution.py:470
  224.8 1.9 collective-permute-done.41.refs_4_
  227.6 1.5 collective-permute-start.42
  229.8 2.4 collective-permute-done.42.refs_2_
  232.2 3.9 %collective-permute-done.44.refs_6_ = f32[264,512]{1,0:T(8,128)S(1)} collective-permute-done((f32[264,512]{1,0:T(8,128)S(1)}, f32[264,512]{1,0:T(8,128)S(1)}, u32[]{:S(2)}, u32[]{:S(2)}) %collective-permute-start.44) | collective-permute-done | bytes 540704 | tf_op jit(solution)/shard_map/ppermute | solution.py:445
  236.7 4.5 %collective-permute-start.48 = (f32[264,512]{1,0:T(8,128)S(1)}, f32[264,512]{1,0:T(8,128)S(1)}, u32[]{:S(2)}, u32[]{:S(2)}) collective-permute-start(f32[264,512]{1,0:T(8,128)S(1)} %get-tuple-element.119.refs_0_), channel_id=1, source_target_pairs={{0,96},{1,13},{2,98},{3,15},{4,100},{5,9},{6,102},{7,11},{8,104},{... | collective-permute-start | bytes 1622024 | tf_op jit(solution)/shard_map/ppermute | solution.py:445
  241.2 1.4 collective-permute-start.45
  242.6 6.1 %collective-permute-done.45.refs_1_.refs_2_ = f32[256,256]{1,0:T(8,128)S(1)} collective-permute-done((f32[256,256]{1,0:T(8,128)S(1)}, f32[256,256]{1,0:T(8,128)S(1)}, u32[]{:S(2)}, u32[]{:S(2)}) %collective-permute-start.45) | collective-permute-done | bytes 262176 | tf_op jit(solution)/shard_map/ppermute | solution.py:434
  249.4 4.2 %collective-permute-start.51 = (f32[256,512]{1,0:T(8,128)S(1)}, f32[256,512]{1,0:T(8,128)S(1)}, u32[]{:S(2)}, u32[]{:S(2)}) collective-permute-start(f32[256,512]{1,0:T(8,128)S(1)} %shard_map.154.refs_0_), channel_id=1, source_target_pairs={{0,12},{1,97},{2,14},{3,99},{4,0},{5,101},{6,2},{7,103},{8,4},{9,1... | collective-permute-start | bytes 1572872 | tf_op jit(solution)/shard_map/ppermute | solution.py:445
  253.6 2.0 collective-permute-start.50
  257.5 1.6 shard_map.153.refs_4_
  259.1 1.6 collective-permute-done.51.refs_3_
  260.6 2.6 collective-permute-done.50.refs_2_
  263.2 5.5 %collective-permute-done.49.refs_1_ = f32[256,512]{1,0:T(8,128)S(1)} collective-permute-done((f32[256,512]{1,0:T(8,128)S(1)}, f32[256,512]{1,0:T(8,128)S(1)}, u32[]{:S(2)}, u32[]{:S(2)}) %collective-permute-start.49) | collective-permute-done | bytes 524320 | tf_op jit(solution)/shard_map/ppermute | solution.py:445
  271.1 2.3 collective-permute-done.52.refs_2_
  273.4 2.1 shard_map.156
  (108 shorter events, 37.9 us)
Async XLA Ops:
  1.9 11.2 %collective-permute-start.1 = (f32[128,256]{1,0:T(8,128)S(1)}, f32[128,256]{1,0:T(8,128)S(1)}, u32[]{:S(2)}, u32[]{:S(2)}) collective-permute-start(f32[128,256]{1,0:T(8,128)S(1)} %dynamic-slice_bitcast_fusion.2), channel_id=1, source_target_pairs={{32,0},{64,32},{96,64},{33,1},{65,33},{97,65},{34,2},{66,34},{98,6... | collective-permute-start | bytes 393224 | tf_op jit(solution)/shard_map/ppermute | solution.py:466
  3.2 9.9 %collective-permute-start = (f32[256,256]{1,0:T(8,128)S(1)}, f32[256,256]{1,0:T(8,128)S(1)}, u32[]{:S(2)}, u32[]{:S(2)}) collective-permute-start(f32[256,256]{1,0:T(8,128)S(1)} %dynamic-slice_bitcast_fusion.1), channel_id=1, source_target_pairs={{0,32},{32,64},{64,96},{1,33},{33,65},{65,97},{2,34},{34,66},{66,9... | collective-permute-start | bytes 786440 | tf_op jit(solution)/shard_map/ppermute | solution.py:466
  12.9 19.2 %copy-start.4 = (f32[2,1,512,512]{3,2,1,0:T(8,128)S(1)}, f32[2,1,512,512]{3,2,1,0:T(8,128)}, u32[]{:S(2)}) copy-start(f32[2,1,512,512]{3,2,1,0:T(8,128)} %param.14) | copy-start | bytes 6291460
  12.9 19.2 %copy-start.5 = (bf16[512,512]{1,0:T(8,128)(2,1)S(1)}, bf16[512,512]{1,0:T(8,128)(2,1)}, u32[]{:S(2)}) copy-start(bf16[512,512]{1,0:T(8,128)(2,1)} %constant.148.clone.refs_6_.refs_8_.refs_10_) | copy-start | bytes 1572868
  12.9 19.2 %copy-start.6 = (bf16[512,512]{1,0:T(8,128)(2,1)S(1)}, bf16[512,512]{1,0:T(8,128)(2,1)}, u32[]{:S(2)}) copy-start(bf16[512,512]{1,0:T(8,128)(2,1)} %constant.147.clone.refs_5_.refs_7_.refs_9_) | copy-start | bytes 1572868
  13.0 19.2 %copy-start.7 = (bf16[512,512]{1,0:T(8,128)(2,1)S(1)}, bf16[512,512]{1,0:T(8,128)(2,1)}, u32[]{:S(2)}) copy-start(bf16[512,512]{1,0:T(8,128)(2,1)} %constant.146.clone.refs_4_.refs_6_.refs_8_) | copy-start | bytes 1572868
  13.0 19.2 %copy-start.8 = (bf16[512,512]{1,0:T(8,128)(2,1)S(1)}, bf16[512,512]{1,0:T(8,128)(2,1)}, u32[]{:S(2)}) copy-start(bf16[512,512]{1,0:T(8,128)(2,1)} %constant.145.clone.refs_3_.refs_5_.refs_7_) | copy-start | bytes 1572868
  13.9 12.8 %collective-permute-start.2 = (f32[512,256]{1,0:T(8,128)S(1)}, f32[512,256]{1,0:T(8,128)S(1)}, u32[]{:S(2)}, u32[]{:S(2)}) collective-permute-start(f32[512,256]{1,0:T(8,128)S(1)} %get-tuple-element.63), channel_id=1, source_target_pairs={{0,4},{4,8},{8,12},{12,16},{16,20},{20,24},{24,28},{1,5},{5,9},{9,... | collective-permute-start | bytes 1572872 | tf_op jit(solution)/shard_map/ppermute | solution.py:466
  17.1 7.9 %collective-permute-start.3 = (f32[512,128]{1,0:T(8,128)S(1)}, f32[512,128]{1,0:T(8,128)S(1)}, u32[]{:S(2)}, u32[]{:S(2)}) collective-permute-start(f32[512,128]{1,0:T(8,128)S(1)} %get-tuple-element.65), channel_id=1, source_target_pairs={{4,0},{8,4},{12,8},{16,12},{20,16},{24,20},{28,24},{5,1},{9,5},{13... | collective-permute-start | bytes 786440 | tf_op jit(solution)/shard_map/ppermute | solution.py:466
  27.4 4.8 %collective-permute-start.4 = (f32[512,512]{1,0:T(8,128)S(1)}, f32[512,512]{1,0:T(8,128)S(1)}, u32[]{:S(2)}, u32[]{:S(2)}) collective-permute-start(f32[512,512]{1,0:T(8,128)S(1)} %shard_map.132.refs_0_), channel_id=1, source_target_pairs={{0,1},{1,0},{2,3},{3,2},{4,5},{5,4},{6,7},{7,6},{8,9},{9,8},{10,11... | collective-permute-start | bytes 3145736 | tf_op jit(solution)/shard_map/ppermute | solution.py:430
  37.4 5.1 %copy-start.3 = (f32[1,512,512]{2,1,0:T(8,128)S(1)}, f32[1,512,512]{2,1,0:T(8,128)}, u32[]{:S(2)}) copy-start(f32[1,512,512]{2,1,0:T(8,128)} %param.15) | copy-start | bytes 3145732
  37.4 2.0 collective-permute-start.5
  39.5 15.1 %collective-permute-start.6 = (f32[264,512]{1,0:T(8,128)S(1)}, f32[264,512]{1,0:T(8,128)S(1)}, u32[]{:S(2)}, u32[]{:S(2)}) collective-permute-start(f32[264,512]{1,0:T(8,128)S(1)} %add.57), channel_id=1, source_target_pairs={{0,2},{2,0},{1,3},{3,1},{4,6},{6,4},{5,7},{7,5},{8,10},{10,8},{9,1... | collective-permute-start | bytes 1622024 | tf_op jit(solution)/shard_map/ppermute | solution.py:434
  42.5 15.2 %copy-start.9 = (bf16[512,512]{1,0:T(8,128)(2,1)S(1)}, bf16[512,512]{1,0:T(8,128)(2,1)}, u32[]{:S(2)}) copy-start(bf16[512,512]{1,0:T(8,128)(2,1)} %constant.152.clone.refs_12_) | copy-start | bytes 1572868
  42.5 15.2 %copy-start.10 = (bf16[512,512]{1,0:T(8,128)(2,1)S(1)}, bf16[512,512]{1,0:T(8,128)(2,1)}, u32[]{:S(2)}) copy-start(bf16[512,512]{1,0:T(8,128)(2,1)} %constant.151.clone.refs_11_) | copy-start | bytes 1572868
  42.5 15.2 %copy-start.11 = (bf16[512,512]{1,0:T(8,128)(2,1)S(1)}, bf16[512,512]{1,0:T(8,128)(2,1)}, u32[]{:S(2)}) copy-start(bf16[512,512]{1,0:T(8,128)(2,1)} %constant.150.clone.refs_10_) | copy-start | bytes 1572868
  42.5 15.2 %copy-start.12 = (bf16[512,512]{1,0:T(8,128)(2,1)S(1)}, bf16[512,512]{1,0:T(8,128)(2,1)}, u32[]{:S(2)}) copy-start(bf16[512,512]{1,0:T(8,128)(2,1)} %constant.149.clone.refs_9_) | copy-start | bytes 1572868
  54.9 2.8 %collective-permute-start.7 = (f32[256,512]{1,0:T(8,128)S(1)}, f32[256,512]{1,0:T(8,128)S(1)}, u32[]{:S(2)}, u32[]{:S(2)}) collective-permute-start(f32[256,512]{1,0:T(8,128)S(1)} %fusion.5.refs_3_), channel_id=1, source_target_pairs={{0,1},{1,0},{2,3},{3,2},{4,5},{5,4},{6,7},{7,6},{8,9},{9,8},{10,11... | collective-permute-start | bytes 1572872 | tf_op jit(solution)/shard_map/ppermute | solution.py:430
  64.2 2.7 collective-permute-start.8
  64.7 6.0 %collective-permute-start.12 = (f32[512,512]{1,0:T(8,128)S(1)}, f32[512,512]{1,0:T(8,128)S(1)}, u32[]{:S(2)}, u32[]{:S(2)}) collective-permute-start(f32[512,512]{1,0:T(8,128)S(1)} %get-tuple-element.78), channel_id=1, source_target_pairs={{0,1},{1,0},{2,3},{3,2},{4,5},{5,4},{6,7},{7,6},{8,9},{9,8},{10,11... | collective-permute-start | bytes 3145736 | tf_op jit(solution)/shard_map/ppermute | solution.py:430
  67.6 14.7 %collective-permute-start.9 = (f32[256,512]{1,0:T(8,128)S(1)}, f32[256,512]{1,0:T(8,128)S(1)}, u32[]{:S(2)}, u32[]{:S(2)}) collective-permute-start(f32[256,512]{1,0:T(8,128)S(1)} %get-tuple-element.73.refs_3_), channel_id=1, source_target_pairs={{0,2},{2,0},{1,3},{3,1},{4,6},{6,4},{5,7},{7,5},{8,10},{10,8},{9,1... | collective-permute-start | bytes 1572872 | tf_op jit(solution)/shard_map/ppermute | solution.py:434
  71.3 11.7 %collective-permute-start.13 = (f32[264,512]{1,0:T(8,128)S(1)}, f32[264,512]{1,0:T(8,128)S(1)}, u32[]{:S(2)}, u32[]{:S(2)}) collective-permute-start(f32[264,512]{1,0:T(8,128)S(1)} %get-tuple-element.81), channel_id=1, source_target_pairs={{0,4},{1,33},{2,6},{3,35},{4,8},{5,37},{6,10},{7,39},{8,12},{9,41}... | collective-permute-start | bytes 1622024 | tf_op jit(solution)/shard_map/ppermute | solution.py:445
  73.4 16.0 %collective-permute-start.14 = (f32[264,512]{1,0:T(8,128)S(1)}, f32[264,512]{1,0:T(8,128)S(1)}, u32[]{:S(2)}, u32[]{:S(2)}) collective-permute-start(f32[264,512]{1,0:T(8,128)S(1)} %get-tuple-element.82), channel_id=1, source_target_pairs={{0,8},{1,65},{2,10},{3,67},{4,12},{5,69},{6,14},{7,71},{8,0},{9,73... | collective-permute-start | bytes 1622024 | tf_op jit(solution)/shard_map/ppermute | solution.py:445
  76.7 12.8 %collective-permute-start.15 = (f32[264,512]{1,0:T(8,128)S(1)}, f32[264,512]{1,0:T(8,128)S(1)}, u32[]{:S(2)}, u32[]{:S(2)}) collective-permute-start(f32[264,512]{1,0:T(8,128)S(1)} %get-tuple-element.83), channel_id=1, source_target_pairs={{0,12},{1,97},{2,14},{3,99},{4,0},{5,101},{6,2},{7,103},{8,4},{9,1... | collective-permute-start | bytes 1622024 | tf_op jit(solution)/shard_map/ppermute | solution.py:445
  90.1 12.4 %collective-permute-start.16 = (f32[264,512]{1,0:T(8,128)S(1)}, f32[264,512]{1,0:T(8,128)S(1)}, u32[]{:S(2)}, u32[]{:S(2)}) collective-permute-start(f32[264,512]{1,0:T(8,128)S(1)} %shard_map.139.refs_3_), channel_id=1, source_target_pairs={{0,32},{1,17},{2,34},{3,19},{4,36},{5,21},{6,38},{7,23},{8,40},{9,... | collective-permute-start | bytes 1622024 | tf_op jit(solution)/shard_map/ppermute | solution.py:445
  93.4 7.9 %collective-permute-start.10 = (f32[256,256]{1,0:T(8,128)S(1)}, f32[256,256]{1,0:T(8,128)S(1)}, u32[]{:S(2)}, u32[]{:S(2)}) collective-permute-start(f32[256,256]{1,0:T(8,128)S(1)} %get-tuple-element.75.refs_4_), channel_id=1, source_target_pairs={{0,28},{4,0},{8,4},{12,8},{16,12},{20,16},{24,20},{28,24},{1,29},{... | collective-permute-start | bytes 786440 | tf_op jit(solution)/shard_map/ppermute | solution.py:470
  94.6 6.0 %collective-permute-start.11 = (f32[256,128]{1,0:T(8,128)S(1)}, f32[256,128]{1,0:T(8,128)S(1)}, u32[]{:S(2)}, u32[]{:S(2)}) collective-permute-start(f32[256,128]{1,0:T(8,128)S(1)} %get-tuple-element.76), channel_id=1, source_target_pairs={{0,4},{4,8},{8,12},{12,16},{16,20},{20,24},{24,28},{28,0},{1,5},{5... | collective-permute-start | bytes 393224 | tf_op jit(solution)/shard_map/ppermute | solution.py:470
  103.3 8.6 %collective-permute-start.19 = (f32[264,512]{1,0:T(8,128)S(1)}, f32[264,512]{1,0:T(8,128)S(1)}, u32[]{:S(2)}, u32[]{:S(2)}) collective-permute-start(f32[264,512]{1,0:T(8,128)S(1)} %get-tuple-element.87.refs_5_), channel_id=1, source_target_pairs={{0,16},{1,5},{2,18},{3,7},{4,20},{5,1},{6,22},{7,3},{8,24},{9,13},... | collective-permute-start | bytes 1622024 | tf_op jit(solution)/shard_map/ppermute | solution.py:445
  103.4 4.6 %collective-permute-start.17 = (f32[192,256]{1,0:T(8,128)S(1)}, f32[192,256]{1,0:T(8,128)S(1)}, u32[]{:S(2)}, u32[]{:S(2)}) collective-permute-start(f32[192,256]{1,0:T(8,128)S(1)} %get-tuple-element.85), channel_id=1, source_target_pairs={{0,32},{32,0},{64,96},{96,64},{1,33},{33,1},{65,97},{97,65},{2,34}... | collective-permute-start | bytes 589832 | tf_op jit(solution)/shard_map/ppermute | solution.py:475
  104.7 3.3 %collective-permute-start.18 = (f32[192,256]{1,0:T(8,128)S(1)}, f32[192,256]{1,0:T(8,128)S(1)}, u32[]{:S(2)}, u32[]{:S(2)}) collective-permute-start(f32[192,256]{1,0:T(8,128)S(1)} %get-tuple-element.86), channel_id=1, source_target_pairs={{32,64},{64,32},{33,65},{65,33},{34,66},{66,34},{35,67},{67,35},{3... | collective-permute-start | bytes 589832 | tf_op jit(solution)/shard_map/ppermute | solution.py:476
  112.6 8.3 %collective-permute-start.20 = (f32[256,256]{1,0:T(8,128)S(1)}, f32[256,256]{1,0:T(8,128)S(1)}, u32[]{:S(2)}, u32[]{:S(2)}) collective-permute-start(f32[256,256]{1,0:T(8,128)S(1)} %get-tuple-element.89), channel_id=1, source_target_pairs={{0,4},{4,8},{8,12},{12,16},{16,20},{20,24},{24,28},{28,0},{1,5},{5... | collective-permute-start | bytes 786440 | tf_op jit(solution)/shard_map/ppermute | solution.py:470
  112.7 6.5 %collective-permute-start.21 = (f32[256,128]{1,0:T(8,128)S(1)}, f32[256,128]{1,0:T(8,128)S(1)}, u32[]{:S(2)}, u32[]{:S(2)}) collective-permute-start(f32[256,128]{1,0:T(8,128)S(1)} %get-tuple-element.91), channel_id=1, source_target_pairs={{0,28},{4,0},{8,4},{12,8},{16,12},{20,16},{24,20},{28,24},{1,29},{... | collective-permute-start | bytes 393224 | tf_op jit(solution)/shard_map/ppermute | solution.py:470
  117.3 12.5 %collective-permute-start.25 = (f32[264,512]{1,0:T(8,128)S(1)}, f32[264,512]{1,0:T(8,128)S(1)}, u32[]{:S(2)}, u32[]{:S(2)}) collective-permute-start(f32[264,512]{1,0:T(8,128)S(1)} %get-tuple-element.92.refs_0_), channel_id=1, source_target_pairs={{0,96},{1,13},{2,98},{3,15},{4,100},{5,9},{6,102},{7,11},{8,104},{... | collective-permute-start | bytes 1622024 | tf_op jit(solution)/shard_map/ppermute | solution.py:445
  121.6 12.7 %collective-permute-start.22 = (f32[256,512]{1,0:T(8,128)S(1)}, f32[256,512]{1,0:T(8,128)S(1)}, u32[]{:S(2)}, u32[]{:S(2)}) collective-permute-start(f32[256,512]{1,0:T(8,128)S(1)} %shard_map.142.refs_2_.refs_0_), channel_id=1, source_target_pairs={{0,2},{2,0},{1,3},{3,1},{4,6},{6,4},{5,7},{7,5},{8,10},{10,8},{9,1... | collective-permute-start | bytes 1572872 | tf_op jit(solution)/shard_map/ppermute | solution.py:434
  130.4 14.0 %collective-permute-start.28 = (f32[256,512]{1,0:T(8,128)S(1)}, f32[256,512]{1,0:T(8,128)S(1)}, u32[]{:S(2)}, u32[]{:S(2)}) collective-permute-start(f32[256,512]{1,0:T(8,128)S(1)} %shard_map.143.refs_0_), channel_id=1, source_target_pairs={{0,12},{1,97},{2,14},{3,99},{4,0},{5,101},{6,2},{7,103},{8,4},{9,1... | collective-permute-start | bytes 1572872 | tf_op jit(solution)/shard_map/ppermute | solution.py:445
  132.7 11.7 %collective-permute-start.27 = (f32[256,512]{1,0:T(8,128)S(1)}, f32[256,512]{1,0:T(8,128)S(1)}, u32[]{:S(2)}, u32[]{:S(2)}) collective-permute-start(f32[256,512]{1,0:T(8,128)S(1)} %shard_map.143.refs_0_), channel_id=1, source_target_pairs={{0,8},{1,65},{2,10},{3,67},{4,12},{5,69},{6,14},{7,71},{8,0},{9,73... | collective-permute-start | bytes 1572872 | tf_op jit(solution)/shard_map/ppermute | solution.py:445
  133.8 14.0 %collective-permute-start.26 = (f32[256,512]{1,0:T(8,128)S(1)}, f32[256,512]{1,0:T(8,128)S(1)}, u32[]{:S(2)}, u32[]{:S(2)}) collective-permute-start(f32[256,512]{1,0:T(8,128)S(1)} %shard_map.143.refs_0_), channel_id=1, source_target_pairs={{0,4},{1,33},{2,6},{3,35},{4,8},{5,37},{6,10},{7,39},{8,12},{9,41}... | collective-permute-start | bytes 1572872 | tf_op jit(solution)/shard_map/ppermute | solution.py:445
  134.3 13.5 %collective-permute-start.24 = (f32[256,512]{1,0:T(8,128)S(1)}, f32[256,512]{1,0:T(8,128)S(1)}, u32[]{:S(2)}, u32[]{:S(2)}) collective-permute-start(f32[256,512]{1,0:T(8,128)S(1)} %collective-permute-done.22.refs_1_), channel_id=1, source_target_pairs={{0,1},{1,0},{2,3},{3,2},{4,5},{5,4},{6,7},{7,6},{8,9},{9,8},{10,11... | collective-permute-start | bytes 1572872 | tf_op jit(solution)/shard_map/ppermute | solution.py:430
  148.5 3.5 %collective-permute-start.29 = (f32[512,512]{1,0:T(8,128)S(1)}, f32[512,512]{1,0:T(8,128)S(1)}, u32[]{:S(2)}, u32[]{:S(2)}) collective-permute-start(f32[512,512]{1,0:T(8,128)S(1)} %get-tuple-element.94), channel_id=1, source_target_pairs={{0,1},{1,0},{2,3},{3,2},{4,5},{5,4},{6,7},{7,6},{8,9},{9,8},{10,11... | collective-permute-start | bytes 3145736 | tf_op jit(solution)/shard_map/ppermute | solution.py:430
  148.9 3.1 %collective-permute-start.23 = (f32[256,512]{1,0:T(8,128)S(1)}, f32[256,512]{1,0:T(8,128)S(1)}, u32[]{:S(2)}, u32[]{:S(2)}) collective-permute-start(f32[256,512]{1,0:T(8,128)S(1)} %shard_map.142.refs_2_.refs_0_), channel_id=1, source_target_pairs={{0,1},{1,0},{2,3},{3,2},{4,5},{5,4},{6,7},{7,6},{8,9},{9,8},{10,11... | collective-permute-start | bytes 1572872 | tf_op jit(solution)/shard_map/ppermute | solution.py:430
  167.6 2.0 collective-permute-start.30
  169.7 15.1 %collective-permute-start.31 = (f32[264,512]{1,0:T(8,128)S(1)}, f32[264,512]{1,0:T(8,128)S(1)}, u32[]{:S(2)}, u32[]{:S(2)}) collective-permute-start(f32[264,512]{1,0:T(8,128)S(1)} %add.59), channel_id=1, source_target_pairs={{0,2},{2,0},{1,3},{3,1},{4,6},{6,4},{5,7},{7,5},{8,10},{10,8},{9,1... | collective-permute-start | bytes 1622024 | tf_op jit(solution)/shard_map/ppermute | solution.py:434
  185.1 2.8 %collective-permute-start.32 = (f32[256,512]{1,0:T(8,128)S(1)}, f32[256,512]{1,0:T(8,128)S(1)}, u32[]{:S(2)}, u32[]{:S(2)}) collective-permute-start(f32[256,512]{1,0:T(8,128)S(1)} %fusion.2.refs_3_), channel_id=1, source_target_pairs={{0,1},{1,0},{2,3},{3,2},{4,5},{5,4},{6,7},{7,6},{8,9},{9,8},{10,11... | collective-permute-start | bytes 1572872 | tf_op jit(solution)/shard_map/ppermute | solution.py:430
  194.2 2.7 collective-permute-start.33
  194.6 4.6 %collective-permute-start.37 = (f32[512,512]{1,0:T(8,128)S(1)}, f32[512,512]{1,0:T(8,128)S(1)}, u32[]{:S(2)}, u32[]{:S(2)}) collective-permute-start(f32[512,512]{1,0:T(8,128)S(1)} %get-tuple-element.108), channel_id=1, source_target_pairs={{0,1},{1,0},{2,3},{3,2},{4,5},{5,4},{6,7},{7,6},{8,9},{9,8},{10,11... | collective-permute-start | bytes 3145736 | tf_op jit(solution)/shard_map/ppermute | solution.py:430
  197.6 14.7 %collective-permute-start.34 = (f32[256,512]{1,0:T(8,128)S(1)}, f32[256,512]{1,0:T(8,128)S(1)}, u32[]{:S(2)}, u32[]{:S(2)}) collective-permute-start(f32[256,512]{1,0:T(8,128)S(1)} %get-tuple-element.103.refs_3_), channel_id=1, source_target_pairs={{0,2},{2,0},{1,3},{3,1},{4,6},{6,4},{5,7},{7,5},{8,10},{10,8},{9,1... | collective-permute-start | bytes 1572872 | tf_op jit(solution)/shard_map/ppermute | solution.py:434
  199.9 13.1 %collective-permute-start.38 = (f32[264,512]{1,0:T(8,128)S(1)}, f32[264,512]{1,0:T(8,128)S(1)}, u32[]{:S(2)}, u32[]{:S(2)}) collective-permute-start(f32[264,512]{1,0:T(8,128)S(1)} %get-tuple-element.111), channel_id=1, source_target_pairs={{0,4},{1,33},{2,6},{3,35},{4,8},{5,37},{6,10},{7,39},{8,12},{9,41}... | collective-permute-start | bytes 1622024 | tf_op jit(solution)/shard_map/ppermute | solution.py:445
  200.7 15.2 %collective-permute-start.39 = (f32[264,512]{1,0:T(8,128)S(1)}, f32[264,512]{1,0:T(8,128)S(1)}, u32[]{:S(2)}, u32[]{:S(2)}) collective-permute-start(f32[264,512]{1,0:T(8,128)S(1)} %get-tuple-element.112), channel_id=1, source_target_pairs={{0,8},{1,65},{2,10},{3,67},{4,12},{5,69},{6,14},{7,71},{8,0},{9,73... | collective-permute-start | bytes 1622024 | tf_op jit(solution)/shard_map/ppermute | solution.py:445
  203.4 12.7 %collective-permute-start.40 = (f32[264,512]{1,0:T(8,128)S(1)}, f32[264,512]{1,0:T(8,128)S(1)}, u32[]{:S(2)}, u32[]{:S(2)}) collective-permute-start(f32[264,512]{1,0:T(8,128)S(1)} %get-tuple-element.113), channel_id=1, source_target_pairs={{0,12},{1,97},{2,14},{3,99},{4,0},{5,101},{6,2},{7,103},{8,4},{9,1... | collective-permute-start | bytes 1622024 | tf_op jit(solution)/shard_map/ppermute | solution.py:445
  216.7 10.0 %collective-permute-start.41 = (f32[264,512]{1,0:T(8,128)S(1)}, f32[264,512]{1,0:T(8,128)S(1)}, u32[]{:S(2)}, u32[]{:S(2)}) collective-permute-start(f32[264,512]{1,0:T(8,128)S(1)} %shard_map.150.refs_3_), channel_id=1, source_target_pairs={{0,32},{1,17},{2,34},{3,19},{4,36},{5,21},{6,38},{7,23},{8,40},{9,... | collective-permute-start | bytes 1622024 | tf_op jit(solution)/shard_map/ppermute | solution.py:445
  217.1 7.8 %collective-permute-start.35 = (f32[256,256]{1,0:T(8,128)S(1)}, f32[256,256]{1,0:T(8,128)S(1)}, u32[]{:S(2)}, u32[]{:S(2)}) collective-permute-start(f32[256,256]{1,0:T(8,128)S(1)} %get-tuple-element.105.refs_4_), channel_id=1, source_target_pairs={{0,28},{4,0},{8,4},{12,8},{16,12},{20,16},{24,20},{28,24},{1,29},{... | collective-permute-start | bytes 786440 | tf_op jit(solution)/shard_map/ppermute | solution.py:470
  218.8 6.0 %collective-permute-start.36 = (f32[256,128]{1,0:T(8,128)S(1)}, f32[256,128]{1,0:T(8,128)S(1)}, u32[]{:S(2)}, u32[]{:S(2)}) collective-permute-start(f32[256,128]{1,0:T(8,128)S(1)} %get-tuple-element.106), channel_id=1, source_target_pairs={{0,4},{4,8},{8,12},{12,16},{16,20},{20,24},{24,28},{28,0},{1,5},{5... | collective-permute-start | bytes 393224 | tf_op jit(solution)/shard_map/ppermute | solution.py:470
  227.5 8.6 %collective-permute-start.44 = (f32[264,512]{1,0:T(8,128)S(1)}, f32[264,512]{1,0:T(8,128)S(1)}, u32[]{:S(2)}, u32[]{:S(2)}) collective-permute-start(f32[264,512]{1,0:T(8,128)S(1)} %get-tuple-element.117.refs_5_), channel_id=1, source_target_pairs={{0,16},{1,5},{2,18},{3,7},{4,20},{5,1},{6,22},{7,3},{8,24},{9,13},... | collective-permute-start | bytes 1622024 | tf_op jit(solution)/shard_map/ppermute | solution.py:445
  227.6 4.6 %collective-permute-start.42 = (f32[192,256]{1,0:T(8,128)S(1)}, f32[192,256]{1,0:T(8,128)S(1)}, u32[]{:S(2)}, u32[]{:S(2)}) collective-permute-start(f32[192,256]{1,0:T(8,128)S(1)} %get-tuple-element.115), channel_id=1, source_target_pairs={{0,32},{32,0},{64,96},{96,64},{1,33},{33,1},{65,97},{97,65},{2,34}... | collective-permute-start | bytes 589832 | tf_op jit(solution)/shard_map/ppermute | solution.py:475
  229.1 3.1 %collective-permute-start.43 = (f32[192,256]{1,0:T(8,128)S(1)}, f32[192,256]{1,0:T(8,128)S(1)}, u32[]{:S(2)}, u32[]{:S(2)}) collective-permute-start(f32[192,256]{1,0:T(8,128)S(1)} %get-tuple-element.116), channel_id=1, source_target_pairs={{32,64},{64,32},{33,65},{65,33},{34,66},{66,34},{35,67},{67,35},{3... | collective-permute-start | bytes 589832 | tf_op jit(solution)/shard_map/ppermute | solution.py:476
  236.7 12.0 %collective-permute-start.48 = (f32[264,512]{1,0:T(8,128)S(1)}, f32[264,512]{1,0:T(8,128)S(1)}, u32[]{:S(2)}, u32[]{:S(2)}) collective-permute-start(f32[264,512]{1,0:T(8,128)S(1)} %get-tuple-element.119.refs_0_), channel_id=1, source_target_pairs={{0,96},{1,13},{2,98},{3,15},{4,100},{5,9},{6,102},{7,11},{8,104},{... | collective-permute-start | bytes 1622024 | tf_op jit(solution)/shard_map/ppermute | solution.py:445
  241.2 7.5 %collective-permute-start.45 = (f32[256,256]{1,0:T(8,128)S(1)}, f32[256,256]{1,0:T(8,128)S(1)}, u32[]{:S(2)}, u32[]{:S(2)}) collective-permute-start(f32[256,256]{1,0:T(8,128)S(1)} %get-tuple-element.118.refs_0_), channel_id=1, source_target_pairs={{0,2},{2,0},{1,3},{3,1},{4,6},{6,4},{5,7},{7,5},{8,10},{10,8},{9,1... | collective-permute-start | bytes 786440 | tf_op jit(solution)/shard_map/ppermute | solution.py:434
  249.4 11.2 %collective-permute-start.51 = (f32[256,512]{1,0:T(8,128)S(1)}, f32[256,512]{1,0:T(8,128)S(1)}, u32[]{:S(2)}, u32[]{:S(2)}) collective-permute-start(f32[256,512]{1,0:T(8,128)S(1)} %shard_map.154.refs_0_), channel_id=1, source_target_pairs={{0,12},{1,97},{2,14},{3,99},{4,0},{5,101},{6,2},{7,103},{8,4},{9,1... | collective-permute-start | bytes 1572872 | tf_op jit(solution)/shard_map/ppermute | solution.py:445
  253.6 9.6 %collective-permute-start.50 = (f32[256,512]{1,0:T(8,128)S(1)}, f32[256,512]{1,0:T(8,128)S(1)}, u32[]{:S(2)}, u32[]{:S(2)}) collective-permute-start(f32[256,512]{1,0:T(8,128)S(1)} %shard_map.154.refs_0_), channel_id=1, source_target_pairs={{0,8},{1,65},{2,10},{3,67},{4,12},{5,69},{6,14},{7,71},{8,0},{9,73... | collective-permute-start | bytes 1572872 | tf_op jit(solution)/shard_map/ppermute | solution.py:445
  255.5 13.2 %collective-permute-start.49 = (f32[256,512]{1,0:T(8,128)S(1)}, f32[256,512]{1,0:T(8,128)S(1)}, u32[]{:S(2)}, u32[]{:S(2)}) collective-permute-start(f32[256,512]{1,0:T(8,128)S(1)} %shard_map.154.refs_0_), channel_id=1, source_target_pairs={{0,4},{1,33},{2,6},{3,35},{4,8},{5,37},{6,10},{7,39},{8,12},{9,41}... | collective-permute-start | bytes 1572872 | tf_op jit(solution)/shard_map/ppermute | solution.py:445
  255.5 1.5 collective-permute-start.46
  255.6 1.9 collective-permute-start.47
  270.6 2.8 %collective-permute-start.52 = (f32[512,512]{1,0:T(8,128)S(1)}, f32[512,512]{1,0:T(8,128)S(1)}, u32[]{:S(2)}, u32[]{:S(2)}) collective-permute-start(f32[512,512]{1,0:T(8,128)S(1)} %get-tuple-element.121), channel_id=1, source_target_pairs={{0,1},{1,0},{2,3},{3,2},{4,5},{5,4},{6,7},{7,6},{8,9},{9,8},{10,11... | collective-permute-start | bytes 3145736 | tf_op jit(solution)/shard_map/ppermute | solution.py:430
  273.4 2.1 copy-start.1
  (2 other events, 2.5 us)
